TPU v7x, 32 devices: a whole 2x2x4 slice. The times are simulated.
32 devices in a mesh: gx: 8 (over z, y), gy: 4 (over x, core).
Axes of the slice: x: 2, y: 2, z: 4, core: 2. Of those that a mesh axis runs over, the one named last changes fastest.
Arguments:
- pressure: float32 [32, 256, 128], P('gx', 'gy'), may hold values from 0.5 to 2
- sat_water: float32 [32, 256, 128], P('gx', 'gy'), may hold values from 0.15 to 0.45
- sat_gas: float32 [32, 256, 128], P('gx', 'gy'), may hold values from 0.05 to 0.35
- pore_volume: float32 [32, 256, 128], P('gx', 'gy'), may hold values from 0.05 to 0.5
- mass_old: float32 [3, 32, 256, 128], P(None, 'gx', 'gy'), may hold values from -1.5 to 1.5
- transmissibility: float32 [3, 32, 256, 128], P(None, 'gx', 'gy'), may hold values from 0.1 to 3
- upwind: int32 [3, 3, 32, 256, 128], P(None, None, 'gx', 'gy'), may hold values from 0 to 1
Outputs:
- residual: float32 [3, 32, 256, 128], P(None, 'gx', 'gy')
- diag_block: float32 [9, 32, 256, 128], P(None, 'gx', 'gy')
- lower_block: float32 [3, 9, 32, 256, 128], P(None, None, 'gx', 'gy')
- upper_block: float32 [3, 9, 32, 256, 128], P(None, None, 'gx', 'gy')
- pressure_rows: float32 [7, 32, 256, 128], P(None, 'gx', 'gy')
- prolongator: float32 [7, 32, 256, 128], P(None, 'gx', 'gy')
- coarse_rhs: float32 [16, 128, 128], P('gx', 'gy')
All inputs are finite; a program needn't handle non-finite values.
Results may differ from a plain program's by a relative error of at most 0.0001.
Values sent between devices are 32-bit elements; how exact they have to be, the bound alone decides.
A program may use at most 64 MiB of HBM per device.

v0:
```python
import jax
import jax.numpy as jnp
from jax import lax
from jax.sharding import PartitionSpec as P

comp_water = 0.05
comp_oil = 0.1
rock_comp = 0.02
gas_ratio = 0.3
visc_water = 0.5
visc_oil = 2.0
visc_gas = 0.2
head_flat = (0.0, 0.0, 0.0)
head_depth = (0.1, 0.08, 0.02)
time_step = 0.5
damping = 2.0 / 3.0


def passed_along(value, axis, steps):
    count = lax.axis_size(axis)
    first, last = (max(0, -steps), min(count, count - steps))
    return lax.ppermute(value, axis, [(source, source + steps) for source in range(first, last)])


def extended(value, sides, width):
    for axis, dim in sides:
        size, length = (lax.axis_size(axis), value.shape[dim])
        up = [(i, (i + 1) % size) for i in range(size - 1)]
        down = [(j, i) for i, j in up]
        last = lax.slice_in_dim(value, length - width, length, axis=dim)
        first = lax.slice_in_dim(value, 0, width, axis=dim)
        before = lax.ppermute(last, axis, up)
        after = lax.ppermute(first, axis, down)
        value = jnp.concatenate([before, value, after], axis=dim)
    return value


def volumes(states):
    press = states[0]
    water = states[1]
    gas_sat = states[2]
    oil_sat = 1.0 - water - gas_sat
    b_water = 1.0 + comp_water * press
    b_oil = 1.0 + comp_oil * press
    return (press, water, gas_sat, oil_sat, b_water, b_oil, press)


def mobility(states):
    press, water, gas_sat, oil_sat, b_water, b_oil, b_gas = volumes(states)
    moving = jnp.stack(
        [
            water * water * b_water / visc_water,
            oil_sat * oil_sat * b_oil / visc_oil,
            gas_sat * gas_sat * b_gas / visc_gas,
        ]
    )
    return (moving, gas_ratio * press)


def face_flux(lower_state, upper_state, trans, upwind, head):
    mob_lower, solved_lower = mobility(lower_state)
    mob_upper, solved_upper = mobility(upper_state)
    chosen = upwind * mob_lower + (1.0 - upwind) * mob_upper
    drop = lower_state[0] - upper_state[0]
    heads = jnp.array(head, jnp.float32).reshape(3, 1, 1, 1)
    phases = trans[None] * chosen * (drop[None] + heads)
    solved = upwind[1] * solved_lower + (1.0 - upwind[1]) * solved_upper
    return jnp.stack([phases[0], phases[1], phases[2] + solved * phases[1]])


def unit_rows(template):
    return [
        jnp.stack(
            [
                jnp.ones_like(template[0]) if column == row else jnp.zeros_like(template[0])
                for column in range(3)
            ]
        )
        for row in range(3)
    ]


def face_terms(lower_state, upper_state, trans, upwind, head):
    fluxes, pullback = jax.vjp(
        lambda first, second: face_flux(first, second, trans, upwind, head),
        lower_state,
        upper_state,
    )
    by_lower = []
    by_upper = []
    for cotangent in unit_rows(fluxes):
        wrt_lower, wrt_upper = pullback(cotangent)
        by_lower.append(wrt_lower)
        by_upper.append(wrt_upper)
    return (fluxes, jnp.concatenate(by_lower, 0), jnp.concatenate(by_upper, 0))


def accumulate(states, pore_volume):
    press, water, gas_sat, oil_sat, b_water, b_oil, b_gas = volumes(states)
    porosity = pore_volume * (1.0 + rock_comp * press)
    return jnp.stack(
        [
            porosity * b_water * water,
            porosity * b_oil * oil_sat,
            porosity * (b_gas * gas_sat + gas_ratio * press * b_oil * oil_sat),
        ]
    )


def accumulation_terms(states, pore_volume):
    masses, pullback = jax.vjp(lambda first: accumulate(first, pore_volume), states)
    rows = [pullback(cotangent)[0] for cotangent in unit_rows(masses)]
    return (masses, jnp.concatenate(rows, 0))


def impes_weights(states):
    press, water, gas_sat, oil_sat, b_water, b_oil, b_gas = volumes(states)
    return jnp.stack([1.0 / b_water, 1.0 / b_oil - gas_ratio, 1.0 / b_gas])


def cut_layer(field, dimension, first_index, last_index):
    return lax.slice_in_dim(field, first_index, last_index, axis=dimension)


def raise_up(field, upper_face, dimension):
    count = field.shape[dimension]
    return jnp.concatenate([cut_layer(field, dimension, 1, count), upper_face], dimension)


def sink_down(field, lower_face, dimension):
    count = field.shape[dimension]
    return jnp.concatenate([lower_face, cut_layer(field, dimension, 0, count - 1)], dimension)


def face_field(states, below, dimension, start, trans, upwind, head):
    lower_state = sink_down(states, below, dimension)
    positions = start + lax.broadcasted_iota(jnp.int32, trans.shape, dimension - 1)
    trans_live = jnp.where(positions > 0, trans, jnp.zeros_like(trans))
    return face_terms(lower_state, states, trans_live, upwind, head)


def assemble(masses, acc_block, mass_old, faces_all, tops_all):
    residual = (masses - mass_old) / time_step
    diagonal = acc_block / time_step
    lowers = []
    uppers = []
    for direction in range(3):
        fluxes, by_lower, by_upper = faces_all[direction]
        flux_top, lower_top, upper_top = tops_all[direction]
        dimension = direction + 1
        residual = residual - fluxes + raise_up(fluxes, flux_top, dimension)
        diagonal = diagonal - by_upper + raise_up(by_lower, lower_top, dimension)
        lowers.append(-by_lower)
        uppers.append(raise_up(by_upper, upper_top, dimension))
    return (residual, diagonal, lowers, uppers)


def pressure_section(weight, acc_block, diagonal, lowers, uppers, odd_x, odd_y):

    def column(block):
        return jnp.sum(weight * block[0::3], axis=0)

    press_diag = column(diagonal)
    press_lower = [column(block) for block in lowers]
    press_upper = [column(block) for block in uppers]
    accum = column(acc_block) / time_step
    divisor = jnp.abs(press_diag) + accum
    for entry in press_lower + press_upper:
        divisor = divisor + jnp.abs(entry)
    scale = damping / divisor
    nothing = jnp.zeros_like(odd_x)
    same_lower = [odd_x, odd_y, nothing]
    same_upper = [1.0 - odd_x, 1.0 - odd_y, nothing]
    inside = press_diag
    for direction in range(3):
        inside = (
            inside
            + same_lower[direction] * press_lower[direction]
            + same_upper[direction] * press_upper[direction]
        )
    own_weight = 1.0 - scale * inside
    near_lower = [
        -scale * press_lower[direction] * (1.0 - same_lower[direction]) for direction in range(3)
    ]
    near_upper = [
        -scale * press_upper[direction] * (1.0 - same_upper[direction]) for direction in range(3)
    ]
    rows_out = jnp.stack([press_diag] + press_lower + press_upper)
    prolong = jnp.stack([own_weight] + near_lower + near_upper)
    return (rows_out, prolong)


def contributions(prolong, residual, weight):
    reduced = jnp.sum(weight * residual, axis=0)
    shares = prolong * reduced[None]
    layer_z = jnp.zeros_like(reduced[:, :, 0:1])
    local_sum = shares[0] + raise_up(shares[3], layer_z, 2) + sink_down(shares[6], layer_z, 2)
    sideways = jnp.stack([shares[1], shares[4], shares[2], shares[5]])
    return (local_sum, sideways)


def block_sum(field):
    span_a, span_b, span_c = field.shape[-3:]
    shaped = field.reshape(field.shape[:-3] + (span_a // 2, 2, span_b // 2, 2, span_c))
    return jnp.sum(shaped, axis=(-4, -2))


def split_terms(received):
    return (received[0:3], received[3:12], received[12:21])


def body(pressure, sat_water, sat_gas, pore_volume, mass_old, transmissibility, upwind):
    span_x, span_y, depth = pressure.shape
    states = jnp.stack([pressure, sat_water, sat_gas])
    masses, acc_block = accumulation_terms(states, pore_volume)
    weight = impes_weights(states)
    flags = upwind.astype(jnp.float32)
    below_x = passed_along(cut_layer(states, 1, span_x - 1, span_x), "gx", 1)
    below_y = passed_along(cut_layer(states, 2, span_y - 1, span_y), "gy", 1)
    start_x = lax.axis_index("gx") * span_x
    start_y = lax.axis_index("gy") * span_y
    faces_x = face_field(states, below_x, 1, start_x, transmissibility[0], flags[0], head_flat)
    faces_y = face_field(states, below_y, 2, start_y, transmissibility[1], flags[1], head_flat)
    below_z = jnp.zeros_like(cut_layer(states, 3, 0, 1))
    faces_z = face_field(states, below_z, 3, 0, transmissibility[2], flags[2], head_depth)
    packed_x = jnp.concatenate([cut_layer(part, 1, 0, 1) for part in faces_x], 0)
    top_x = split_terms(passed_along(packed_x, "gx", -1))
    packed_y = jnp.concatenate([cut_layer(part, 2, 0, 1) for part in faces_y], 0)
    top_y = split_terms(passed_along(packed_y, "gy", -1))
    zero_nine = jnp.zeros_like(cut_layer(acc_block, 3, 0, 1))
    top_z = (below_z, zero_nine, zero_nine)
    residual, diagonal, lowers, uppers = assemble(
        masses, acc_block, mass_old, [faces_x, faces_y, faces_z], [top_x, top_y, top_z]
    )
    odd_x = (lax.broadcasted_iota(jnp.int32, pressure.shape, 0) % 2).astype(jnp.float32)
    odd_y = (lax.broadcasted_iota(jnp.int32, pressure.shape, 1) % 2).astype(jnp.float32)
    rows_out, prolong = pressure_section(weight, acc_block, diagonal, lowers, uppers, odd_x, odd_y)
    local_sum, sideways = contributions(prolong, residual, weight)
    wider = extended(sideways, (("gx", 1), ("gy", 2)), 1)
    total = (
        local_sum
        + wider[0, 2:, 1:-1]
        + wider[1, :-2, 1:-1]
        + wider[2, 1:-1, 2:]
        + wider[3, 1:-1, :-2]
    )
    coarse = block_sum(total)
    return (residual, diagonal, jnp.stack(lowers), jnp.stack(uppers), rows_out, prolong, coarse)


def solution(mesh):
    in_specs = (
        P("gx", "gy", None),
        P("gx", "gy", None),
        P("gx", "gy", None),
        P("gx", "gy", None),
        P(None, "gx", "gy", None),
        P(None, "gx", "gy", None),
        P(None, None, "gx", "gy", None),
    )
    out_specs = (
        P(None, "gx", "gy", None),
        P(None, "gx", "gy", None),
        P(None, None, "gx", "gy", None),
        P(None, None, "gx", "gy", None),
        P(None, "gx", "gy", None),
        P(None, "gx", "gy", None),
        P("gx", "gy", None),
    )
    return jax.shard_map(body, mesh=mesh, in_specs=in_specs, out_specs=out_specs, check_vma=False)
```

profile of v0, /device:TPU:9, one launch (start us, length us, event | category | flops | bytes accessed | tf_op | source)
XLA Modules:
  0.0 71.5 jit_solution(3015926395527350723)
XLA Ops:
  0.6 1.1 %pad_maximum_fusion.15 = f32[3,4,64,128]{3,2,1,0:T(8,128)S(1)} fusion(f32[1,4,64,128]{3,2,1,0:T(8,128)} %bitcast.776, f32[1,4,64,128]{3,2,1,0:T(8,128)} %bitcast.774, f32[1,4,64,128]{3,2,1,0:T(8,128)} %bitcast.778), kind=kLoop, calls=%fused_computation.88 | loop fusion | flops 196608 | bytes 786432 | tf_op jit(solution)/shard_map/stack | solution.py:214
  1.8 3.3 %collective-permute-start = (f32[3,1,64,128]{3,2,1,0:T(8,128)S(1)}, f32[3,1,64,128]{3,2,1,0:T(8,128)S(1)}, u32[]{:S(2)}, u32[]{:S(2)}) collective-permute-start(f32[3,1,64,128]{3,2,1,0:T(8,128)S(1)} %slice.335), channel_id=1, source_target_pairs={{0,4},{4,8},{8,12},{12,16},{16,20},{20,24},{24,28},{1,5},{5,9},{9,... | collective-permute-start | bytes 294920 | tf_op jit(solution)/shard_map/ppermute | solution.py:22
  5.1 0.8 %pad_maximum_fusion.51 = f32[3,4,1,128]{3,2,1,0:T(1,128)S(1)} fusion(f32[1,4,64,128]{3,2,1,0:T(8,128)} %bitcast.777, f32[1,4,64,128]{3,2,1,0:T(8,128)} %bitcast.775, f32[1,4,64,128]{3,2,1,0:T(8,128)} %bitcast.779), kind=kLoop, calls=%fused_computation.581 | loop fusion | flops 3072 | bytes 399360 | tf_op jit(solution)/shard_map/slice | solution.py:122
  5.8 3.9 %collective-permute-start.2 = (f32[3,4,1,128]{3,2,1,0:T(1,128)S(1)}, f32[3,4,1,128]{3,2,1,0:T(1,128)S(1)}, u32[]{:S(2)}, u32[]{:S(2)}) collective-permute-start(f32[3,4,1,128]{3,2,1,0:T(1,128)S(1)} %pad_maximum_fusion.51), channel_id=1, source_target_pairs={{0,1},{1,2},{2,3},{4,5},{5,6},{6,7},{8,9},{9,10},{10,11},{12,13},{... | collective-permute-start | bytes 18440 | tf_op jit(solution)/shard_map/ppermute | solution.py:22
  9.9 0.2 multiply_multiply_fusion.9
  10.3 0.2 collective-permute-done.2
  10.5 0.6 copy-done.2
  11.1 0.2 multiply_bitcast_fusion
  11.3 0.5 copy-done.12
  11.8 0.2 subtract_multiply_fusion.2
  12.0 0.2 subtract_multiply_fusion
  12.5 0.2 subtract_multiply_fusion.6
  12.6 0.7 copy-done
  13.4 0.2 fusion.147
  13.7 0.8 %multiply_add_fusion.5 = (f32[1,4,64,128]{3,2,1,0:T(8,128)S(1)}, f32[1,4,64,128]{3,2,1,0:T(8,128)S(1)}, f32[1,4,64,128]{3,2,1,0:T(8,128)S(1)}, f32[1,4,64,128]{3...) fusion(f32[3,4,64,128]{3,2,1,0:T(8,128)S(1)} %get-tuple-element, ...), kind=kLoop, calls=%fused_computation.430 | loop fusion | flops 3080192 | bytes 2487296 | tf_op jit(solution)/shard_map/transpose(jvp())/add_any | solution.py:42
  14.6 0.6 add_bitcast_fusion.11
  15.2 0.2 multiply_reduce_fusion.10
  15.6 0.3 multiply_add_fusion.37
  16.0 0.2 subtract_multiply_fusion.3
  16.2 0.2 multiply_add_fusion.23
  16.3 0.2 multiply_add_fusion.21
  16.6 0.2 multiply_reduce_fusion.13
  16.8 0.2 multiply_add_fusion.42
  17.2 0.2 multiply_add_fusion.33
  17.4 0.2 multiply_reduce_fusion.16
  17.6 0.2 multiply_add_fusion.46
  17.9 0.2 add_bitcast_fusion.15
  18.1 0.2 add_bitcast_fusion.13
  18.3 0.3 fusion.151
  18.6 0.2 add_bitcast_fusion.2
  19.9 0.3 pad_maximum_fusion.4
  20.2 1.9 %collective-permute-start.3 = (f32[21,4,1,128]{3,2,1,0:T(1,128)S(1)}, f32[21,4,1,128]{3,2,1,0:T(1,128)S(1)}, u32[]{:S(2)}, u32[]{:S(2)}) collective-permute-start(f32[21,4,1,128]{3,2,1,0:T(1,128)S(1)} %pad_maximum_fusion.44), channel_id=1, source_target_pairs={{1,0},{2,1},{3,2},{5,4},{6,5},{7,6},{9,8},{10,9},{11,10},{13,12},{... | collective-permute-start | bytes 129032 | tf_op jit(solution)/shard_map/ppermute | solution.py:22
  22.4 0.3 pad_maximum_fusion.2
  22.7 0.7 copy-done.3
  23.5 0.9 %slice-done = f32[9,1,64,128]{3,2,1,0:T(8,128)S(1)} async-done(((f32[9,4,64,128]{3,2,1,0:T(8,128)}), f32[9,1,64,128]{3,2,1,0:T(8,128)S(1)}, s32[]{:S(2)}) %slice-start) | async-done | bytes 294936 | tf_op jit(solution)/shard_map/slice | solution.py:122
  24.5 3.2 %collective-permute-start.1 = (f32[21,1,64,128]{3,2,1,0:T(8,128)S(1)}, f32[21,1,64,128]{3,2,1,0:T(8,128)S(1)}, u32[]{:S(2)}, u32[]{:S(2)}) collective-permute-start(f32[21,1,64,128]{3,2,1,0:T(8,128)S(1)} %pad_maximum_fusion.11), channel_id=1, source_target_pairs={{4,0},{8,4},{12,8},{16,12},{20,16},{24,20},{28,24},{5,1},{9,5},{13... | collective-permute-start | bytes 2064392 | tf_op jit(solution)/shard_map/ppermute | solution.py:22
  28.0 0.4 slice.386
  28.4 0.1 pad_bitcast_fusion
  28.5 0.2 fusion.4
  28.8 0.3 pad_maximum_fusion.8
  29.7 2.1 %pad_maximum_fusion = f32[3,9,4,64,128]{4,3,2,1,0:T(8,128)} fusion(f32[1,9,4,64,128]{4,3,2,1,0:T(8,128)S(1)} %maximum_negate_fusion.2, f32[1,9,4,64,128]{4,3,2,1,0:T(8,128)S(1)} %maximum_negate_fusion.1, f32[1,9,4,64,128]{4,3,2,1,0:T(8,128)S(1)} %maximum_negate_fusion), kind=kLoop, calls=%fused_computation | loop fusion | flops 1769472 | bytes 7077888 | tf_op jit(solution)/shard_map/stack | solution.py:248
  32.1 0.4 slice.381
  32.5 0.2 pad_maximum_fusion.10
  32.7 0.4 copy-done.10
  33.1 9.1 %collective-permute-done.1 = f32[21,1,64,128]{3,2,1,0:T(8,128)S(1)} collective-permute-done((f32[21,1,64,128]{3,2,1,0:T(8,128)S(1)}, f32[21,1,64,128]{3,2,1,0:T(8,128)S(1)}, u32[]{:S(2)}, u32[]{:S(2)}) %collective-permute-start.1) | collective-permute-done | bytes 688160 | tf_op jit(solution)/shard_map/ppermute | solution.py:22
  42.3 0.3 pad_maximum_fusion.9
  42.6 1.0 %fusion.3 = f32[9,4,64,128]{3,2,1,0:T(8,128)S(1)} fusion(f32[9,1,64,128]{3,2,1,0:T(8,128)S(1)} %get-tuple-element.135, f32[9,3,64,128]{3,2,1,0:T(8,128)S(1)} %slice.377, f32[9,4,1,128]{3,2,1,0:T(1,128)S(1)} %get-tuple-element.224, f32[9,4,63,128]{3,2,1,0:T(8,128)S(1)} %slice.379, f32[9,4,64,127]{3,2,1,0:T(8,128)S(1)} %slice.381, ...), kind=kLoop, calls=%fused_computation.23 | loop fusion | flops 5013504 | bytes 9427968 | tf_op jit(solution)/shard_map/add | solution.py:152
  43.6 0.3 multiply_reduce_fusion.1
  43.9 0.7 copy-done.4
  44.6 0.3 copy-done.7
  44.8 1.3 %multiply_reduce_fusion = (f32[4,64,128]{2,1,0:T(8,128)S(1)}, f32[4,64,128]{2,1,0:T(8,128)S(1)}, f32[4,64,128]{2,1,0:T(8,128)S(1)}, f32[4,64,128]{2,1,0:T(8,128)S(1)}, f32[3,4,64,128]{3,2,1,0:T(8,128)}) fusion(f32[1,4,64,128]{3,2,1,0:T(8,128)S(1)} %get-tuple-element.221, f32[1,4,64,128]{3,2,1,0:T(8,128)S(1)} %get-tuple-element.220, ...), kind=kLoop, calls=%fused_computation.100 | loop fusion | flops 2326528 | bytes 5633024 | tf_op jit(solution)/shard_map/reduce_sum | solution.py:194
  46.2 0.2 fusion.91
  47.0 0.7 copy-done.5
  47.7 0.3 copy-done.11
  48.1 3.5 %collective-permute-start.4 = (f32[4,1,64,128]{3,2,1,0:T(8,128)S(1)}, f32[4,1,64,128]{3,2,1,0:T(8,128)S(1)}, u32[]{:S(2)}, u32[]{:S(2)}) collective-permute-start(f32[4,1,64,128]{3,2,1,0:T(8,128)S(1)} %get-tuple-element.137), channel_id=1, source_target_pairs={{4,0},{8,4},{12,8},{16,12},{20,16},{24,20},{28,24},{5,1},{9,5},{13... | collective-permute-start | bytes 393224 | tf_op jit(solution)/shard_map/ppermute | solution.py:33
  51.6 2.0 %collective-permute-start.5 = (f32[4,1,64,128]{3,2,1,0:T(8,128)S(1)}, f32[4,1,64,128]{3,2,1,0:T(8,128)S(1)}, u32[]{:S(2)}, u32[]{:S(2)}) collective-permute-start(f32[4,1,64,128]{3,2,1,0:T(8,128)S(1)} %get-tuple-element.136), channel_id=1, source_target_pairs={{0,4},{4,8},{8,12},{12,16},{16,20},{20,24},{24,28},{1,5},{5,9},{9,... | collective-permute-start | bytes 393224 | tf_op jit(solution)/shard_map/ppermute | solution.py:32
  53.6 0.2 fusion.189
  53.8 1.2 %collective-permute-done.4 = f32[4,1,64,128]{3,2,1,0:T(8,128)S(1)} collective-permute-done((f32[4,1,64,128]{3,2,1,0:T(8,128)S(1)}, f32[4,1,64,128]{3,2,1,0:T(8,128)S(1)}, u32[]{:S(2)}, u32[]{:S(2)}) %collective-permute-start.4) | collective-permute-done | bytes 131104 | tf_op jit(solution)/shard_map/ppermute | solution.py:33
  55.0 4.3 %collective-permute-done.5 = f32[4,1,64,128]{3,2,1,0:T(8,128)S(1)} collective-permute-done((f32[4,1,64,128]{3,2,1,0:T(8,128)S(1)}, f32[4,1,64,128]{3,2,1,0:T(8,128)S(1)}, u32[]{:S(2)}, u32[]{:S(2)}) %collective-permute-start.5) | collective-permute-done | bytes 131104 | tf_op jit(solution)/shard_map/ppermute | solution.py:32
  59.3 6.3 %collective-permute-start.7 = (f32[4,6,1,128]{3,2,1,0:T(1,128)S(1)}, f32[4,6,1,128]{3,2,1,0:T(1,128)S(1)}, u32[]{:S(2)}, u32[]{:S(2)}) collective-permute-start(f32[4,6,1,128]{3,2,1,0:T(1,128)S(1)} %get-tuple-element.101), channel_id=1, source_target_pairs={{0,1},{1,2},{2,3},{4,5},{5,6},{6,7},{8,9},{9,10},{10,11},{12,13},{... | collective-permute-start | bytes 36872 | tf_op jit(solution)/shard_map/ppermute | solution.py:32
  65.7 1.9 %collective-permute-start.6 = (f32[4,6,1,128]{3,2,1,0:T(1,128)S(1)}, f32[4,6,1,128]{3,2,1,0:T(1,128)S(1)}, u32[]{:S(2)}, u32[]{:S(2)}) collective-permute-start(f32[4,6,1,128]{3,2,1,0:T(1,128)S(1)} %get-tuple-element.100), channel_id=1, source_target_pairs={{1,0},{2,1},{3,2},{5,4},{6,5},{7,6},{9,8},{10,9},{11,10},{13,12},{... | collective-permute-start | bytes 36872 | tf_op jit(solution)/shard_map/ppermute | solution.py:33
  67.6 2.0 %pad_maximum_fusion.1 = f32[3,9,4,64,128]{4,3,2,1,0:T(8,128)} fusion(f32[1,9,4,64,128]{4,3,2,1,0:T(8,128)S(1)} %pad_bitcast_fusion, f32[1,9,4,64,128]{4,3,2,1,0:T(8,128)S(1)} %fusion.189, f32[1,9,4,64,128]{4,3,2,1,0:T(8,128)S(1)} %get-tuple-element.87), kind=kLoop, calls=%fused_computation.1 | loop fusion | flops 1769472 | bytes 7077888 | tf_op jit(solution)/shard_map/stack | solution.py:248
  69.7 0.9 %collective-permute-done.6 = f32[4,6,1,128]{3,2,1,0:T(1,128)S(1)} collective-permute-done((f32[4,6,1,128]{3,2,1,0:T(1,128)S(1)}, f32[4,6,1,128]{3,2,1,0:T(1,128)S(1)}, u32[]{:S(2)}, u32[]{:S(2)}) %collective-permute-start.6) | collective-permute-done | bytes 12320 | tf_op jit(solution)/shard_map/ppermute | solution.py:33
  70.8 0.7 reduce_sum.234
  (117 shorter events, 4.6 us)
Async XLA Ops:
  0.6 9.5 %copy-start.8 = (f32[3,4,64,128]{3,2,1,0:T(8,128)S(1)}, f32[3,4,64,128]{3,2,1,0:T(8,128)}, u32[]{:S(2)}) copy-start(f32[3,4,64,128]{3,2,1,0:T(8,128)} %param.15) | copy-start | bytes 1179652
  1.8 8.5 %copy-start.6 = (s32[3,3,4,64,128]{4,3,2,1,0:T(8,128)S(1)}, s32[3,3,4,64,128]{4,3,2,1,0:T(8,128)}, u32[]{:S(2)}) copy-start(s32[3,3,4,64,128]{4,3,2,1,0:T(8,128)} %param.16) | copy-start | bytes 3538948
  1.8 8.8 %collective-permute-start = (f32[3,1,64,128]{3,2,1,0:T(8,128)S(1)}, f32[3,1,64,128]{3,2,1,0:T(8,128)S(1)}, u32[]{:S(2)}, u32[]{:S(2)}) collective-permute-start(f32[3,1,64,128]{3,2,1,0:T(8,128)S(1)} %slice.335), channel_id=1, source_target_pairs={{0,4},{4,8},{8,12},{12,16},{16,20},{20,24},{24,28},{1,5},{5,9},{9,... | collective-permute-start | bytes 294920 | tf_op jit(solution)/shard_map/ppermute | solution.py:22
  5.8 4.7 %collective-permute-start.2 = (f32[3,4,1,128]{3,2,1,0:T(1,128)S(1)}, f32[3,4,1,128]{3,2,1,0:T(1,128)S(1)}, u32[]{:S(2)}, u32[]{:S(2)}) collective-permute-start(f32[3,4,1,128]{3,2,1,0:T(1,128)S(1)} %pad_maximum_fusion.51), channel_id=1, source_target_pairs={{0,1},{1,2},{2,3},{4,5},{5,6},{6,7},{8,9},{9,10},{10,11},{12,13},{... | collective-permute-start | bytes 18440 | tf_op jit(solution)/shard_map/ppermute | solution.py:22
  10.2 0.9 %copy-start.2 = (f32[4,64,128]{2,1,0:T(8,128)S(1)}, f32[4,64,128]{2,1,0:T(8,128)}, u32[]{:S(2)}) copy-start(f32[4,64,128]{2,1,0:T(8,128)} %param.10) | copy-start | bytes 393220
  11.1 0.7 copy-start.12
  12.4 0.9 %copy-start = (f32[4,64,128]{2,1,0:T(8,128)S(1)}, f32[4,64,128]{2,1,0:T(8,128)}, u32[]{:S(2)}) copy-start(f32[4,64,128]{2,1,0:T(8,128)} %param.11) | copy-start | bytes 393220
  12.4 1.0 %copy-start.1 = (f32[4,64,128]{2,1,0:T(8,128)S(1)}, f32[4,64,128]{2,1,0:T(8,128)}, u32[]{:S(2)}) copy-start(f32[4,64,128]{2,1,0:T(8,128)} %param.12) | copy-start | bytes 393220
  13.7 0.9 %copy-start.9 = (f32[4,64,128]{2,1,0:T(8,128)S(1)}, f32[4,64,128]{2,1,0:T(8,128)}, u32[]{:S(2)}) copy-start(f32[4,64,128]{2,1,0:T(8,128)} %param.13) | copy-start | bytes 393220
  20.2 12.3 %collective-permute-start.3 = (f32[21,4,1,128]{3,2,1,0:T(1,128)S(1)}, f32[21,4,1,128]{3,2,1,0:T(1,128)S(1)}, u32[]{:S(2)}, u32[]{:S(2)}) collective-permute-start(f32[21,4,1,128]{3,2,1,0:T(1,128)S(1)} %pad_maximum_fusion.44), channel_id=1, source_target_pairs={{1,0},{2,1},{3,2},{5,4},{6,5},{7,6},{9,8},{10,9},{11,10},{13,12},{... | collective-permute-start | bytes 129032 | tf_op jit(solution)/shard_map/ppermute | solution.py:22
  22.4 1.0 %copy-start.3 = (f32[9,4,64,128]{3,2,1,0:T(8,128)}, f32[9,4,64,128]{3,2,1,0:T(8,128)S(1)}, u32[]{:S(2)}) copy-start(f32[9,4,64,128]{3,2,1,0:T(8,128)S(1)} %pad_maximum_fusion.3) | copy-start | bytes 3538948
  23.4 1.0 %slice-start = ((f32[9,4,64,128]{3,2,1,0:T(8,128)}), f32[9,1,64,128]{3,2,1,0:T(8,128)S(1)}, s32[]{:S(2)}) async-start(f32[9,4,64,128]{3,2,1,0:T(8,128)} %copy-done.3), calls=%async_computation | async-start | bytes 589824 | tf_op jit(solution)/shard_map/slice | solution.py:122
  24.5 17.7 %collective-permute-start.1 = (f32[21,1,64,128]{3,2,1,0:T(8,128)S(1)}, f32[21,1,64,128]{3,2,1,0:T(8,128)S(1)}, u32[]{:S(2)}, u32[]{:S(2)}) collective-permute-start(f32[21,1,64,128]{3,2,1,0:T(8,128)S(1)} %pad_maximum_fusion.11), channel_id=1, source_target_pairs={{4,0},{8,4},{12,8},{16,12},{20,16},{24,20},{28,24},{5,1},{9,5},{13... | collective-permute-start | bytes 2064392 | tf_op jit(solution)/shard_map/ppermute | solution.py:22
  32.5 0.6 copy-start.10
  33.1 9.2 %slice-start.1 = ((f32[9,4,64,128]{3,2,1,0:T(8,128)}), f32[9,3,64,128]{3,2,1,0:T(8,128)S(1)}, s32[]{:S(2)}) async-start(f32[9,4,64,128]{3,2,1,0:T(8,128)} %copy-done.3), calls=%async_computation.1 | async-start | bytes 1769472 | tf_op jit(solution)/shard_map/slice | solution.py:122
  43.5 1.0 %copy-start.4 = (f32[9,4,64,128]{3,2,1,0:T(8,128)}, f32[9,4,64,128]{3,2,1,0:T(8,128)S(1)}, u32[]{:S(2)}) copy-start(f32[9,4,64,128]{3,2,1,0:T(8,128)S(1)} %fusion.3) | copy-start | bytes 3538948
  43.5 1.3 %copy-start.7 = (f32[3,4,64,128]{3,2,1,0:T(8,128)S(1)}, f32[3,4,64,128]{3,2,1,0:T(8,128)}, u32[]{:S(2)}) copy-start(f32[3,4,64,128]{3,2,1,0:T(8,128)} %param.14) | copy-start | bytes 1179652
  43.6 1.3 %slice-start.2 = ((f32[21,4,1,128]{3,2,1,0:T(1,128)}), f32[3,4,1,128]{3,2,1,0:T(1,128)S(1)}, s32[]{:S(2)}) async-start(f32[21,4,1,128]{3,2,1,0:T(1,128)} %copy-done.10), calls=%async_computation.2 | async-start | bytes 12288 | tf_op jit(solution)/shard_map/slice | solution.py:209
  46.8 0.9 %copy-start.5 = (f32[7,4,64,128]{3,2,1,0:T(8,128)}, f32[7,4,64,128]{3,2,1,0:T(8,128)S(1)}, u32[]{:S(2)}) copy-start(f32[7,4,64,128]{3,2,1,0:T(8,128)S(1)} %get-tuple-element.206) | copy-start | bytes 2752516
  46.8 1.2 %copy-start.11 = (f32[7,4,64,128]{3,2,1,0:T(8,128)}, f32[7,4,64,128]{3,2,1,0:T(8,128)S(1)}, u32[]{:S(2)}) copy-start(f32[7,4,64,128]{3,2,1,0:T(8,128)S(1)} %get-tuple-element.207) | copy-start | bytes 2752516
  48.1 6.9 %collective-permute-start.4 = (f32[4,1,64,128]{3,2,1,0:T(8,128)S(1)}, f32[4,1,64,128]{3,2,1,0:T(8,128)S(1)}, u32[]{:S(2)}, u32[]{:S(2)}) collective-permute-start(f32[4,1,64,128]{3,2,1,0:T(8,128)S(1)} %get-tuple-element.137), channel_id=1, source_target_pairs={{4,0},{8,4},{12,8},{16,12},{20,16},{24,20},{28,24},{5,1},{9,5},{13... | collective-permute-start | bytes 393224 | tf_op jit(solution)/shard_map/ppermute | solution.py:33
  51.6 7.7 %collective-permute-start.5 = (f32[4,1,64,128]{3,2,1,0:T(8,128)S(1)}, f32[4,1,64,128]{3,2,1,0:T(8,128)S(1)}, u32[]{:S(2)}, u32[]{:S(2)}) collective-permute-start(f32[4,1,64,128]{3,2,1,0:T(8,128)S(1)} %get-tuple-element.136), channel_id=1, source_target_pairs={{0,4},{4,8},{8,12},{12,16},{16,20},{20,24},{24,28},{1,5},{5,9},{9,... | collective-permute-start | bytes 393224 | tf_op jit(solution)/shard_map/ppermute | solution.py:32
  59.3 10.4 %collective-permute-start.7 = (f32[4,6,1,128]{3,2,1,0:T(1,128)S(1)}, f32[4,6,1,128]{3,2,1,0:T(1,128)S(1)}, u32[]{:S(2)}, u32[]{:S(2)}) collective-permute-start(f32[4,6,1,128]{3,2,1,0:T(1,128)S(1)} %get-tuple-element.101), channel_id=1, source_target_pairs={{0,1},{1,2},{2,3},{4,5},{5,6},{6,7},{8,9},{9,10},{10,11},{12,13},{... | collective-permute-start | bytes 36872 | tf_op jit(solution)/shard_map/ppermute | solution.py:32
  65.7 5.0 %collective-permute-start.6 = (f32[4,6,1,128]{3,2,1,0:T(1,128)S(1)}, f32[4,6,1,128]{3,2,1,0:T(1,128)S(1)}, u32[]{:S(2)}, u32[]{:S(2)}) collective-permute-start(f32[4,6,1,128]{3,2,1,0:T(1,128)S(1)} %get-tuple-element.100), channel_id=1, source_target_pairs={{1,0},{2,1},{3,2},{5,4},{6,5},{7,6},{9,8},{10,9},{11,10},{13,12},{... | collective-permute-start | bytes 36872 | tf_op jit(solution)/shard_map/ppermute | solution.py:33
where the time goes:
time: 72 us; the launch traced here: 71.5 us
  starting transfers between devices  26.2 us (36%)
  other arithmetic  20.3 us (28%)
  waiting for transfers between devices  15.7 us (22%)
  local copies, waits for them, and re-layouts  7.6 us (11%)
  between operations  1.67 us (2%)
    ppermute x4, starting transfers between devices, passed_along(): lax.ppermute(value, axis, [(source, source + steps) for source in range(f...  12.4 us
    ppermute x4, waiting for transfers between devices, passed_along(): lax.ppermute(value, axis, [(source, source + steps) for source in range(f...  9.31 us
    ppermute x2, starting transfers between devices, extended(): before = lax.ppermute(last, axis, up)  8.37 us
    ppermute x2, starting transfers between devices, extended(): after = lax.ppermute(first, axis, down)  5.45 us
    unnamed x26, local copies, waits for them, and re-layouts  5.07 us
    ppermute x2, waiting for transfers between devices, extended(): before = lax.ppermute(last, axis, up)  4.32 us
    another operation x2, other arithmetic, body(): jnp.stack(uppers)  2.2 us
    slice x15, local copies, waits for them, and re-layouts, cut_layer(): return lax.slice_in_dim(field, first_index, last_index, axis=dimension)  2.19 us
  transfers between devices with their start and end apart: 8, of which 5 were waited for; matrix products, arithmetic and copies ran while one was open for 12% of the time, Pallas kernels for 0%

commit v1 on v0

v1 whole, which is shorter than its diff:
```python
import jax
import jax.numpy as jnp
from jax import lax
from jax.experimental import pallas as pl
from jax.experimental.pallas import tpu as pltpu
from jax.sharding import PartitionSpec as P

MESH = pl.DeviceIdType.MESH
ROWS = 8
PLACES = (0, 1, 3, 4, 6, 7, 8)


def neighbours():
    found = []
    for axis in ("gx", "gy"):
        here, size = lax.axis_index(axis), lax.axis_size(axis)
        found.append((axis, here - 1, here > 0))
        found.append((axis, here + 1, here < size - 1))
    return found


def meet():
    barrier = pltpu.get_barrier_semaphore()
    for axis, other, there in neighbours():

        @pl.when(there)
        def _():
            pl.semaphore_signal(barrier, inc=1, device_id={axis: other}, device_id_type=MESH)

    peers = sum(there.astype(jnp.int32) for _, _, there in neighbours())
    pl.semaphore_wait(barrier, peers)


def halo_kernel(p, sw, sg, t, u, xlo, xhi, xt, xu, ylo, yhi, yt, yu, send, recv):
    nx, ny, nz = p.shape
    states = (p, sw, sg)
    last = pl.ds(ny - ROWS, ROWS)
    first = pl.ds(0, ROWS)
    x_up = [(s.at[nx - 1], xlo.at[i]) for i, s in enumerate(states)]
    x_down = [(s.at[0], xhi.at[i]) for i, s in enumerate(states)]
    x_down += [(t.at[0, 0], xt), (u.at[0, :, 0], xu)]
    y_up = [(s.at[:, last], ylo.at[i]) for i, s in enumerate(states)]
    y_down = [(s.at[:, first], yhi.at[i]) for i, s in enumerate(states)]
    y_down += [(t.at[1, :, first], yt), (u.at[1, :, :, first], yu)]
    groups = (x_down, x_up, y_down, y_up)
    (_, xl, has_xl), (_, xh, has_xh), (_, yl, has_yl), (_, yh, has_yh) = neighbours()
    routes = (
        ("gx", xl, has_xl, has_xh),
        ("gx", xh, has_xh, has_xl),
        ("gy", yl, has_yl, has_yh),
        ("gy", yh, has_yh, has_yl),
    )
    meet()
    remote = []
    index = 0
    for group, (axis, other, sends, gets) in zip(groups, routes):
        copies = []
        for source, target in group:
            copies.append(
                pltpu.make_async_remote_copy(
                    src_ref=source,
                    dst_ref=target,
                    send_sem=send.at[index],
                    recv_sem=recv.at[index],
                    device_id={axis: other},
                    device_id_type=MESH,
                )
            )
            index += 1
        remote.append(copies)

        @pl.when(sends)
        def _():
            for copy in copies:
                copy.start()

    index = 0
    for group, (axis, other, sends, gets) in zip(groups, routes):

        @pl.when(jnp.logical_not(gets))
        def _():
            for k, (source, target) in enumerate(group):
                pltpu.make_async_copy(source, target, recv.at[index + k]).start()
            for k, (source, target) in enumerate(group):
                pltpu.make_async_copy(source, target, recv.at[index + k]).wait()

        index += len(group)
    for copies, (axis, other, sends, gets) in zip(remote, routes):

        @pl.when(sends)
        def _():
            for copy in copies:
                copy.wait_send()

        @pl.when(gets)
        def _():
            for copy in copies:
                copy.wait_recv()


def cell(p, sw, sg):
    so = 1.0 - sw - sg
    bw = 1.0 + 0.05 * p
    bo = 1.0 + 0.1 * p
    ww, oo, gg = sw * sw, so * so, 5.0 * (sg * sg)
    sob = so * bo
    return dict(
        p=p, sw=sw, sg=sg, so=so, bw=bw, bo=bo, sob=sob, rs=0.3 * p,
        m=(2.0 * ww * bw, 0.5 * so * sob, gg * p),
        mp=(0.1 * ww, 0.05 * oo, gg),
        ms=(4.0 * sw * bw, -sob, 10.0 * sg * p),
    )


def face(low, high, t, flags, heads):
    drop = low["p"] - high["p"]
    ups = [flag > 0 for flag in flags]
    flow, by_low, by_high = [], [], []
    for a in range(3):
        drive = t * (drop + heads[a]) if heads[a] else t * drop
        chosen = jnp.where(ups[a], low["m"][a], high["m"][a])
        moved = t * chosen
        flow.append(drive * chosen)
        from_low = jnp.where(ups[a], drive, 0.0)
        from_high = jnp.where(ups[a], 0.0, drive)
        by_low.append((from_low * low["mp"][a] + moved, from_low * low["ms"][a]))
        by_high.append((from_high * high["mp"][a] - moved, from_high * high["ms"][a]))
    solved = jnp.where(ups[1], low["rs"], high["rs"])
    fluxes = [flow[0], flow[1], flow[2] + solved * flow[1]]
    third = 0.3 * flow[1]
    extra_low = jnp.where(ups[1], third, 0.0)
    extra_high = jnp.where(ups[1], 0.0, third)
    out = []
    for (w, o, g), extra in ((by_low, extra_low), (by_high, extra_high)):
        carried = solved * o[1]
        out.append([w[0], w[1], o[0], o[1], g[0] + solved * o[0] + extra, carried, g[1] + carried])
    return fluxes, out[0], out[1]


def column(weight, entries):
    return weight[0] * entries[0] + weight[1] * entries[2] + weight[2] * entries[4]


def put(ref, lead, x, rows, entries, sign=1.0):
    for place, entry in zip(PLACES, entries):
        ref[lead + (place, x, rows)] = entry if sign > 0 else -entry
    ref[lead + (2, x, rows)] = jnp.zeros_like(entries[0])
    ref[lead + (5, x, rows)] = entries[3] if sign > 0 else -entries[3]


def main_kernel(
    p, sw, sg, pv, old, t, u, xlo, xhi, xt, xu, ylo, yhi, yt, yu,
    res_o, diag_o, low_o, up_o, rows_o, pro_o, coarse_o, sx_o, sy_o,
    ps, pvs, olds, txs, tys, tzs, uxs, uys, uzs,
    res_v, diag_v, low_v, up_v, rows_v, pro_v, own_s, side_s,
    in_sem, out_sem,
):
    nx, ny, nz = p.shape
    steps = ny // ROWS
    inner = pl.ds(ROWS, ny)
    mid = pl.ds(1, nx)
    pairs = []
    for i, s in enumerate((p, sw, sg)):
        pairs += [
            (s, ps.at[i, mid, inner]),
            (xlo.at[i], ps.at[i, 0, inner]),
            (xhi.at[i], ps.at[i, nx + 1, inner]),
            (ylo.at[i], ps.at[i, mid, pl.ds(0, ROWS)]),
            (yhi.at[i], ps.at[i, mid, pl.ds(ROWS + ny, ROWS)]),
        ]
    pairs += [
        (pv, pvs), (old, olds),
        (t.at[0], txs.at[pl.ds(0, nx)]), (xt, txs.at[nx]),
        (t.at[1], tys.at[:, pl.ds(0, ny)]), (yt, tys.at[:, pl.ds(ny, ROWS)]),
        (t.at[2], tzs),
        (u.at[0], uxs.at[:, pl.ds(0, nx)]), (xu, uxs.at[:, nx]),
        (u.at[1], uys.at[:, :, pl.ds(0, ny)]), (yu, uys.at[:, :, pl.ds(ny, ROWS)]),
        (u.at[2], uzs),
    ]
    copies = [pltpu.make_async_copy(a, b, in_sem.at[k]) for k, (a, b) in enumerate(pairs)]
    for copy in copies:
        copy.start()
    for copy in copies:
        copy.wait()

    gx, gy = lax.axis_index("gx"), lax.axis_index("gy")

    @pl.when(gx == 0)
    def _():
        txs[0] = jnp.zeros((ny, nz), jnp.float32)

    @pl.when(gx == lax.axis_size("gx") - 1)
    def _():
        txs[nx] = jnp.zeros((ny, nz), jnp.float32)

    @pl.when(gy == 0)
    def _():
        tys[:, 0:1] = jnp.zeros((nx, 1, nz), jnp.float32)

    @pl.when(gy == lax.axis_size("gy") - 1)
    def _():
        tys[:, ny : ny + 1] = jnp.zeros((nx, 1, nz), jnp.float32)

    side_s[:, 0:ROWS] = jnp.zeros((nx // 2, ROWS, nz), jnp.float32)
    side_s[:, ny + ROWS :] = jnp.zeros((nx // 2, ROWS, nz), jnp.float32)

    lane = lax.broadcasted_iota(jnp.int32, (ROWS, nz), 1)
    odd = lax.broadcasted_iota(jnp.int32, (ROWS, nz), 0) % 2 == 1
    flat, depth = (0.0, 0.0, 0.0), (0.1, 0.08, 0.02)
    outs = ((res_v, res_o), (diag_v, diag_o), (low_v, low_o), (up_v, up_o), (rows_v, rows_o), (pro_v, pro_o))

    def out_copies(j):
        made = []
        rows = pl.ds(pl.multiple_of(j * ROWS, ROWS), ROWS)
        for k, (v, o) in enumerate(outs):
            lead = (slice(None),) * (len(v.shape) - 2)
            made.append(pltpu.make_async_copy(v.at[lead + (rows,)], o.at[lead + (rows,)], out_sem.at[j, k]))
        return made

    def step(j, carry):
        start = pl.multiple_of(j * ROWS, ROWS)
        rows = pl.ds(start, ROWS)
        here = pl.ds(pl.multiple_of(start + ROWS, ROWS), ROWS)
        before = pl.ds(start + ROWS - 1, ROWS)
        after = pl.ds(start + ROWS + 1, ROWS)
        following = pl.ds(start + 1, ROWS)

        def states(x, where):
            return [ps[i, x, where] for i in range(3)]

        def x_face(x, low, high):
            return face(low, high, txs[x, rows], [uxs[a, x, rows] for a in range(3)], flat)

        below, centre = cell(*states(0, here)), cell(*states(1, here))
        x_low = x_face(0, below, centre)
        agg = [None] * (nx // 2)
        side = [None] * (nx // 2)

        def add(items, place, value):
            items[place] = value if items[place] is None else items[place] + value

        for x in range(nx):
            above = cell(*states(x + 2, here))
            x_up = x_face(x + 1, centre, above)
            y_low = face(
                cell(*states(x + 1, before)), centre, tys[x, rows],
                [uys[a, x, rows] for a in range(3)], flat,
            )
            y_up = face(
                centre, cell(*states(x + 1, after)), tys[x, following],
                [uys[a, x, following] for a in range(3)], flat,
            )
            under = cell(*[pltpu.roll(centre[n], 1, 1) for n in ("p", "sw", "sg")])
            z_t = jnp.where(lane > 0, tzs[x, rows], 0.0)
            z_low = face(under, centre, z_t, [uzs[a, x, rows] for a in range(3)], depth)
            z_up = [[pltpu.roll(v, nz - 1, 1) for v in part] for part in z_low]
            lows, ups = (x_low, y_low, z_low), (x_up, y_up, z_up)

            c = centre
            pore = pvs[x, rows]
            phi = pore + 0.02 * pore * c["p"]
            dphi = 0.02 * pore
            water, oil = c["bw"] * c["sw"], c["sob"]
            gas = c["p"] * c["sg"] + c["rs"] * oil
            pob = phi * c["bo"]
            rob = c["rs"] * pob
            acc = [
                dphi * water + 0.05 * phi * c["sw"],
                phi * c["bw"],
                dphi * oil + 0.1 * phi * c["so"],
                -pob,
                dphi * gas + phi * (c["sg"] + 0.3 * oil + 0.1 * c["rs"] * c["so"]),
                -rob,
                phi * c["p"] - rob,
            ]
            acc = [2.0 * v for v in acc]
            mass = (phi * water, phi * oil, phi * gas)
            residual = []
            for k in range(3):
                r = 2.0 * (mass[k] - olds[k, x, rows])
                for d in range(3):
                    r = r - lows[d][0][k] + ups[d][0][k]
                res_v[k, x, rows] = r
                residual.append(r)
            diag = []
            for k in range(7):
                v = acc[k]
                for d in range(3):
                    v = v - lows[d][2][k] + ups[d][1][k]
                diag.append(v)
            put(diag_v, (), x, rows, diag)
            for d in range(3):
                put(low_v, (d,), x, rows, lows[d][1], -1.0)
                put(up_v, (d,), x, rows, ups[d][2])

            weight = (1.0 / c["bw"], 1.0 / c["bo"] - 0.3, 1.0 / c["p"])
            p_diag = column(weight, diag)
            p_low = [-column(weight, lows[d][1]) for d in range(3)]
            p_up = [column(weight, ups[d][2]) for d in range(3)]
            divisor = jnp.abs(p_diag) + column(weight, acc)
            for v in p_low + p_up:
                divisor = divisor + jnp.abs(v)
            scale = (2.0 / 3.0) / divisor
            for k, v in enumerate([p_diag] + p_low + p_up):
                rows_v[k, x, rows] = v
            y_same = jnp.where(odd, p_low[1], p_up[1])
            y_low_other = jnp.where(odd, 0.0, p_low[1])
            y_up_other = jnp.where(odd, p_up[1], 0.0)
            x_same, x_other = (p_low[0], p_up[0]) if x % 2 else (p_up[0], p_low[0])
            own = 1.0 - scale * (p_diag + x_same + y_same)
            minus = -scale
            w_x = minus * x_other
            w_yl, w_yu = minus * y_low_other, minus * y_up_other
            w_zl, w_zu = minus * p_low[2], minus * p_up[2]
            none = jnp.zeros_like(own)
            w_xl, w_xu = (none, w_x) if x % 2 else (w_x, none)
            for k, v in enumerate((own, w_xl, w_yl, w_zl, w_xu, w_yu, w_zu)):
                pro_v[k, x, rows] = v

            reduced = weight[0] * residual[0] + weight[1] * residual[1] + weight[2] * residual[2]
            local = own * reduced + pltpu.roll(w_zl * reduced, nz - 1, 1) + pltpu.roll(w_zu * reduced, 1, 1)
            add(agg, x // 2, local)
            add(side, x // 2, (w_yl + w_yu) * reduced)
            share = w_x * reduced
            if x == 0:
                own_s[nx // 2, rows] = share
            elif x == nx - 1:
                own_s[nx // 2 + 1, rows] = share
            else:
                add(agg, (x + 1) // 2 if x % 2 else (x - 1) // 2, share)
            x_low, centre = x_up, above
        for a in range(nx // 2):
            own_s[a, rows] = agg[a]
            side_s[a, here] = side[a]
        for copy in out_copies(j):
            copy.start()
        return carry

    lax.fori_loop(0, steps, step, 0)

    half = ny // 2
    for a in range(nx // 2):
        coarse_o[a] = (
            own_s[a, pl.ds(0, half, stride=2)]
            + own_s[a, pl.ds(1, half, stride=2)]
            + side_s[a, pl.ds(ROWS + 2, half, stride=2)]
            + side_s[a, pl.ds(ROWS - 1, half, stride=2)]
        )
        sy_o[0, a : a + 1] = side_s[a, ROWS : ROWS + 1]
        sy_o[1, a : a + 1] = side_s[a, ROWS + ny - 1 : ROWS + ny]
    for s in range(2):
        sx_o[s] = own_s[nx // 2 + s, pl.ds(0, half, stride=2)] + own_s[nx // 2 + s, pl.ds(1, half, stride=2)]

    def finish(j, carry):
        for copy in out_copies(j):
            copy.wait()
        return carry

    lax.fori_loop(0, steps, finish, 0)


def share_kernel(coarse, sx, sy, out, gx_in, gy_in, send, recv):
    ax, half, nz = coarse.shape
    (_, xl, has_xl), (_, xh, has_xh), (_, yl, has_yl), (_, yh, has_yh) = neighbours()
    meet()
    routes = (
        (sx.at[0], gx_in.at[0], "gx", xl, has_xl, has_xh),
        (sx.at[1], gx_in.at[1], "gx", xh, has_xh, has_xl),
        (sy.at[0], gy_in.at[0], "gy", yl, has_yl, has_yh),
        (sy.at[1], gy_in.at[1], "gy", yh, has_yh, has_yl),
    )
    copies = []
    for k, (source, target, axis, other, sends, gets) in enumerate(routes):
        copy = pltpu.make_async_remote_copy(
            src_ref=source, dst_ref=target, send_sem=send.at[k], recv_sem=recv.at[k],
            device_id={axis: other}, device_id_type=MESH,
        )
        copies.append(copy)

        @pl.when(sends)
        def _():
            copy.start()

    out[...] = coarse[...]
    for k, (source, target, axis, other, sends, gets) in enumerate(routes):
        copy = copies[k]

        @pl.when(gets)
        def _():
            copy.wait_recv()
            if k == 0:
                out[ax - 1] += gx_in[0]
            elif k == 1:
                out[0] += gx_in[1]
            else:
                place = half - 1 if k == 2 else 0
                for a in range(ax):
                    out[a, place : place + 1] += gy_in[k - 2, a : a + 1]

        @pl.when(sends)
        def _():
            copy.wait_send()


def body(pressure, sat_water, sat_gas, pore_volume, mass_old, transmissibility, upwind):
    nx, ny, nz = pressure.shape
    f32, i32 = jnp.float32, jnp.int32
    anywhere = pl.BlockSpec(memory_space=pl.ANY)
    in_vmem = pl.BlockSpec(memory_space=pltpu.VMEM)
    shape = jax.ShapeDtypeStruct
    halos = pl.pallas_call(
        halo_kernel,
        out_shape=[
            shape((3, ny, nz), f32), shape((3, ny, nz), f32), shape((ny, nz), f32), shape((3, ny, nz), i32),
            shape((3, nx, ROWS, nz), f32), shape((3, nx, ROWS, nz), f32), shape((nx, ROWS, nz), f32),
            shape((3, nx, ROWS, nz), i32),
        ],
        in_specs=[anywhere] * 5,
        out_specs=[anywhere] * 8,
        scratch_shapes=[pltpu.SemaphoreType.DMA((16,)), pltpu.SemaphoreType.DMA((16,))],
        compiler_params=pltpu.CompilerParams(collective_id=0, has_side_effects=True),
        name="halo",
    )(pressure, sat_water, sat_gas, transmissibility, upwind)
    grid = (nx, ny, nz)
    lead = ((3,), (9,), (3, 9), (3, 9), (7,), (7,))
    results = pl.pallas_call(
        main_kernel,
        out_shape=[shape(k + grid, f32) for k in lead]
        + [shape((nx // 2, ny // 2, nz), f32), shape((2, ny // 2, nz), f32), shape((2, nx // 2, nz), f32)],
        in_specs=[anywhere] * 15,
        out_specs=[anywhere] * 6 + [in_vmem] * 3,
        scratch_shapes=[
            pltpu.VMEM((3, nx + 2, ny + 2 * ROWS, nz), f32),
            pltpu.VMEM(grid, f32),
            pltpu.VMEM((3,) + grid, f32),
            pltpu.VMEM((nx + 1, ny, nz), f32),
            pltpu.VMEM((nx, ny + ROWS, nz), f32),
            pltpu.VMEM(grid, f32),
            pltpu.VMEM((3, nx + 1, ny, nz), i32),
            pltpu.VMEM((3, nx, ny + ROWS, nz), i32),
            pltpu.VMEM((3,) + grid, i32),
        ]
        + [pltpu.VMEM(k + grid, f32) for k in lead]
        + [
            pltpu.VMEM((nx // 2 + 2, ny, nz), f32),
            pltpu.VMEM((nx // 2, ny + 2 * ROWS, nz), f32),
            pltpu.SemaphoreType.DMA((27,)),
            pltpu.SemaphoreType.DMA((ny // ROWS, 6)),
        ],
        compiler_params=pltpu.CompilerParams(vmem_limit_bytes=40 * 2**20),
        name="assemble",
    )(pressure, sat_water, sat_gas, pore_volume, mass_old, transmissibility, upwind, *halos)
    *blocks, coarse, sx, sy = results
    coarse = pl.pallas_call(
        share_kernel,
        out_shape=shape(coarse.shape, f32),
        in_specs=[in_vmem] * 3,
        out_specs=in_vmem,
        scratch_shapes=[
            pltpu.VMEM(sx.shape, f32), pltpu.VMEM(sy.shape, f32),
            pltpu.SemaphoreType.DMA((4,)), pltpu.SemaphoreType.DMA((4,)),
        ],
        compiler_params=pltpu.CompilerParams(collective_id=1, has_side_effects=True),
        name="shares",
    )(coarse, sx, sy)
    return (*blocks, coarse)


def solution(mesh):
    cells = P("gx", "gy", None)
    one = P(None, "gx", "gy", None)
    two = P(None, None, "gx", "gy", None)
    return jax.shard_map(
        body,
        mesh=mesh,
        in_specs=(cells, cells, cells, cells, one, one, two),
        out_specs=(one, one, two, two, one, one, cells),
        check_vma=False,
    )
```

time: 72 us -> 44.4 us (0.62)
  the two profiles are of different devices: /device:TPU:9 before, /device:TPU:0 now
where the time goes in v1:
time: 44.4 us; the launch traced here: 43.6 us
  Pallas kernels  26.3 us (59%)
  local copies, waits for them, and re-layouts  16.6 us (37%)
  between operations  0.69 us (2%)
    unnamed x37, local copies, waits for them, and re-layouts  16.6 us
    pallas_call x1, Pallas kernels, body(): pl.pallas_call(halo_kernel, out_shape=[shape((3, ny, nz), f32), shape((3,...  11.1 us
    pallas_call x1, Pallas kernels, body(): pl.pallas_call(share_kernel, out_shape=shape(coarse.shape, f32), in_specs...  8.09 us
    pallas_call x1, Pallas kernels, body(): pl.pallas_call(main_kernel, out_shape=[shape(k + grid, f32) for k in lead...  7.11 us

profile of v1, /device:TPU:0, one launch (start us, length us, event | category | flops | bytes accessed | tf_op | source)
XLA Modules:
  0.0 43.6 jit_solution(7733652135279183224)
XLA Ops:
  0.6 11.1 %halo.1 = (f32[3,64,128]{2,1,0:T(8,128)}, f32[3,64,128]{2,1,0:T(8,128)}, f32[64,128]{1,0:T(8,128)}, s32[3,64,128]{2,1,0:T(8,128)}, f32[3,4,8,128]{3,2,1,0:T(8,12...) custom-call(f32[4,64,128]{2,1,0:T(8,128)} %p.3, f32[4,64,128]{2,1,0:T(8,128)} %sw.3, ...), custom_call_target="tpu_custom_call" | custom-call | tf_op jit(solution)/shard_map/halo/pallas_call | solution.py:411
  11.8 0.0 copy-start
  11.8 1.3 %copy-done = s32[3,3,4,64,128]{4,3,2,1,0:T(8,128)S(1)} copy-done((s32[3,3,4,64,128]{4,3,2,1,0:T(8,128)S(1)}, s32[3,3,4,64,128]{4,3,2,1,0:T(8,128)}, u32[]{:S(2)}) %copy-start) | copy-done | bytes 1179672
  13.0 0.0 copy-start.1
  13.0 1.0 %copy-done.1 = f32[3,4,64,128]{3,2,1,0:T(8,128)S(1)} copy-done((f32[3,4,64,128]{3,2,1,0:T(8,128)S(1)}, f32[3,4,64,128]{3,2,1,0:T(8,128)}, u32[]{:S(2)}) %copy-start.1) | copy-done | bytes 393240
  14.0 0.0 copy-start.2
  14.0 0.9 %copy-done.2 = f32[4,64,128]{2,1,0:T(8,128)S(1)} copy-done((f32[4,64,128]{2,1,0:T(8,128)S(1)}, f32[4,64,128]{2,1,0:T(8,128)}, u32[]{:S(2)}) %copy-start.2) | copy-done | bytes 131096
  14.9 0.0 copy-start.3
  14.9 0.9 %copy-done.3 = f32[4,64,128]{2,1,0:T(8,128)S(1)} copy-done((f32[4,64,128]{2,1,0:T(8,128)S(1)}, f32[4,64,128]{2,1,0:T(8,128)}, u32[]{:S(2)}) %copy-start.3) | copy-done | bytes 131096
  15.8 0.0 copy-start.4
  15.8 0.9 %copy-done.4 = f32[4,64,128]{2,1,0:T(8,128)S(1)} copy-done((f32[4,64,128]{2,1,0:T(8,128)S(1)}, f32[4,64,128]{2,1,0:T(8,128)}, u32[]{:S(2)}) %copy-start.4) | copy-done | bytes 131096
  16.7 0.0 copy-start.5
  16.7 1.0 %copy-done.5 = f32[3,4,64,128]{3,2,1,0:T(8,128)S(1)} copy-done((f32[3,4,64,128]{3,2,1,0:T(8,128)S(1)}, f32[3,4,64,128]{3,2,1,0:T(8,128)}, u32[]{:S(2)}) %copy-start.5) | copy-done | bytes 393240
  17.7 0.0 copy-start.6
  17.7 0.9 %copy-done.6 = f32[4,64,128]{2,1,0:T(8,128)S(1)} copy-done((f32[4,64,128]{2,1,0:T(8,128)S(1)}, f32[4,64,128]{2,1,0:T(8,128)}, u32[]{:S(2)}) %copy-start.6) | copy-done | bytes 131096
  18.6 0.0 copy-start.7
  18.6 0.9 %copy-done.7 = f32[3,64,128]{2,1,0:T(8,128)S(1)} copy-done((f32[3,64,128]{2,1,0:T(8,128)S(1)}, f32[3,64,128]{2,1,0:T(8,128)}, u32[]{:S(2)}) %copy-start.7) | copy-done | bytes 98328
  19.5 0.0 copy-start.8
  19.5 0.9 %copy-done.8 = f32[3,64,128]{2,1,0:T(8,128)S(1)} copy-done((f32[3,64,128]{2,1,0:T(8,128)S(1)}, f32[3,64,128]{2,1,0:T(8,128)}, u32[]{:S(2)}) %copy-start.8) | copy-done | bytes 98328
  20.4 0.0 copy-start.9
  20.4 0.9 %copy-done.9 = s32[3,64,128]{2,1,0:T(8,128)S(1)} copy-done((s32[3,64,128]{2,1,0:T(8,128)S(1)}, s32[3,64,128]{2,1,0:T(8,128)}, u32[]{:S(2)}) %copy-start.9) | copy-done | bytes 98328
  21.3 0.0 copy-start.10
  21.3 0.8 %copy-done.10 = f32[3,4,8,128]{3,2,1,0:T(8,128)S(1)} copy-done((f32[3,4,8,128]{3,2,1,0:T(8,128)S(1)}, f32[3,4,8,128]{3,2,1,0:T(8,128)}, u32[]{:S(2)}) %copy-start.10) | copy-done | bytes 49176
  22.1 0.0 copy-start.11
  22.1 0.8 %copy-done.11 = f32[3,4,8,128]{3,2,1,0:T(8,128)S(1)} copy-done((f32[3,4,8,128]{3,2,1,0:T(8,128)S(1)}, f32[3,4,8,128]{3,2,1,0:T(8,128)}, u32[]{:S(2)}) %copy-start.11) | copy-done | bytes 49176
  22.9 0.0 copy-start.12
  22.9 0.8 %copy-done.12 = s32[3,4,8,128]{3,2,1,0:T(8,128)S(1)} copy-done((s32[3,4,8,128]{3,2,1,0:T(8,128)S(1)}, s32[3,4,8,128]{3,2,1,0:T(8,128)}, u32[]{:S(2)}) %copy-start.12) | copy-done | bytes 49176
  23.7 0.0 copy-start.13
  23.7 0.8 %copy-done.13 = f32[64,128]{1,0:T(8,128)S(1)} copy-done((f32[64,128]{1,0:T(8,128)S(1)}, f32[64,128]{1,0:T(8,128)}, u32[]{:S(2)}) %copy-start.13) | copy-done | bytes 32792
  24.5 0.0 copy-start.16
  24.5 0.7 %copy-done.16 = f32[4,8,128]{2,1,0:T(8,128)S(1)} copy-done((f32[4,8,128]{2,1,0:T(8,128)S(1)}, f32[4,8,128]{2,1,0:T(8,128)}, u32[]{:S(2)}) %copy-start.16) | copy-done | bytes 16408
  25.2 7.1 %assemble.1 = (f32[3,4,64,128]{3,2,1,0:T(8,128)}, f32[9,4,64,128]{3,2,1,0:T(8,128)}, f32[3,9,4,64,128]{4,3,2,1,0:T(8,128)}, f32[3,9,4,64,128]{4,3,2,1,0:T(8,128)...) custom-call(f32[4,64,128]{2,1,0:T(8,128)S(1)} %copy-done.2, ...), custom_call_target="tpu_custom_call" | custom-call | tf_op jit(solution)/shard_map/assemble/pallas_call | solution.py:426
  32.3 0.0 copy-start.14
  32.3 0.6 %copy-done.14 = f32[2,32,128]{2,1,0:T(8,128)} copy-done((f32[2,32,128]{2,1,0:T(8,128)}, f32[2,32,128]{2,1,0:T(8,128)S(1)}, u32[]{:S(2)}) %copy-start.14) | copy-done | bytes 32792
  32.9 0.0 copy-start.15
  32.9 0.6 %copy-done.15 = f32[2,32,128]{2,1,0:T(8,128)} copy-done((f32[2,32,128]{2,1,0:T(8,128)}, f32[2,32,128]{2,1,0:T(8,128)S(1)}, u32[]{:S(2)}) %copy-start.15) | copy-done | bytes 32792
  33.5 0.0 copy-start.17
  33.5 0.6 %copy-done.17 = f32[2,2,128]{2,1,0:T(2,128)} copy-done((f32[2,2,128]{2,1,0:T(2,128)}, f32[2,2,128]{2,1,0:T(2,128)S(1)}, u32[]{:S(2)}) %copy-start.17) | copy-done | bytes 2072
  34.1 8.1 %shares.1 = f32[2,32,128]{2,1,0:T(8,128)} custom-call(f32[2,32,128]{2,1,0:T(8,128)} %copy-done.14, f32[2,32,128]{2,1,0:T(8,128)} %copy-done.15, f32[2,2,128]{2,1,0:T(2,128)} %copy-done.17), custom_call_target="tpu_custom_call" | custom-call | tf_op jit(solution)/shard_map/shares/pallas_call | solution.py:454
  42.2 1.4 %copy.15 = f32[2,32,128]{2,1,0:T(8,128)} copy(f32[2,32,128]{2,1,0:T(8,128)} %shares.1) | data formatting | bytes 65536
Async XLA Ops:
  11.8 1.3 %copy-start = (s32[3,3,4,64,128]{4,3,2,1,0:T(8,128)S(1)}, s32[3,3,4,64,128]{4,3,2,1,0:T(8,128)}, u32[]{:S(2)}) copy-start(s32[3,3,4,64,128]{4,3,2,1,0:T(8,128)} %u.3) | copy-start | bytes 3538948
  13.0 1.0 %copy-start.1 = (f32[3,4,64,128]{3,2,1,0:T(8,128)S(1)}, f32[3,4,64,128]{3,2,1,0:T(8,128)}, u32[]{:S(2)}) copy-start(f32[3,4,64,128]{3,2,1,0:T(8,128)} %t.3) | copy-start | bytes 1179652
  14.0 0.9 %copy-start.2 = (f32[4,64,128]{2,1,0:T(8,128)S(1)}, f32[4,64,128]{2,1,0:T(8,128)}, u32[]{:S(2)}) copy-start(f32[4,64,128]{2,1,0:T(8,128)} %p.3) | copy-start | bytes 393220
  14.9 0.9 %copy-start.3 = (f32[4,64,128]{2,1,0:T(8,128)S(1)}, f32[4,64,128]{2,1,0:T(8,128)}, u32[]{:S(2)}) copy-start(f32[4,64,128]{2,1,0:T(8,128)} %sw.3) | copy-start | bytes 393220
  15.8 0.9 %copy-start.4 = (f32[4,64,128]{2,1,0:T(8,128)S(1)}, f32[4,64,128]{2,1,0:T(8,128)}, u32[]{:S(2)}) copy-start(f32[4,64,128]{2,1,0:T(8,128)} %sg.3) | copy-start | bytes 393220
  16.7 1.0 %copy-start.5 = (f32[3,4,64,128]{3,2,1,0:T(8,128)S(1)}, f32[3,4,64,128]{3,2,1,0:T(8,128)}, u32[]{:S(2)}) copy-start(f32[3,4,64,128]{3,2,1,0:T(8,128)} %old.1) | copy-start | bytes 1179652
  17.7 0.9 %copy-start.6 = (f32[4,64,128]{2,1,0:T(8,128)S(1)}, f32[4,64,128]{2,1,0:T(8,128)}, u32[]{:S(2)}) copy-start(f32[4,64,128]{2,1,0:T(8,128)} %pv.1) | copy-start | bytes 393220
  18.6 0.9 %copy-start.7 = (f32[3,64,128]{2,1,0:T(8,128)S(1)}, f32[3,64,128]{2,1,0:T(8,128)}, u32[]{:S(2)}) copy-start(f32[3,64,128]{2,1,0:T(8,128)} %get-tuple-element.24.xlo) | copy-start | bytes 294916
  19.5 0.9 %copy-start.8 = (f32[3,64,128]{2,1,0:T(8,128)S(1)}, f32[3,64,128]{2,1,0:T(8,128)}, u32[]{:S(2)}) copy-start(f32[3,64,128]{2,1,0:T(8,128)} %get-tuple-element.25.xhi) | copy-start | bytes 294916
  20.4 0.9 %copy-start.9 = (s32[3,64,128]{2,1,0:T(8,128)S(1)}, s32[3,64,128]{2,1,0:T(8,128)}, u32[]{:S(2)}) copy-start(s32[3,64,128]{2,1,0:T(8,128)} %get-tuple-element.27.xu) | copy-start | bytes 294916
  21.3 0.8 %copy-start.10 = (f32[3,4,8,128]{3,2,1,0:T(8,128)S(1)}, f32[3,4,8,128]{3,2,1,0:T(8,128)}, u32[]{:S(2)}) copy-start(f32[3,4,8,128]{3,2,1,0:T(8,128)} %get-tuple-element.28.ylo) | copy-start | bytes 147460
  22.1 0.8 %copy-start.11 = (f32[3,4,8,128]{3,2,1,0:T(8,128)S(1)}, f32[3,4,8,128]{3,2,1,0:T(8,128)}, u32[]{:S(2)}) copy-start(f32[3,4,8,128]{3,2,1,0:T(8,128)} %get-tuple-element.29.yhi) | copy-start | bytes 147460
  22.9 0.8 %copy-start.12 = (s32[3,4,8,128]{3,2,1,0:T(8,128)S(1)}, s32[3,4,8,128]{3,2,1,0:T(8,128)}, u32[]{:S(2)}) copy-start(s32[3,4,8,128]{3,2,1,0:T(8,128)} %get-tuple-element.31.yu) | copy-start | bytes 147460
  23.7 0.8 %copy-start.13 = (f32[64,128]{1,0:T(8,128)S(1)}, f32[64,128]{1,0:T(8,128)}, u32[]{:S(2)}) copy-start(f32[64,128]{1,0:T(8,128)} %get-tuple-element.26.xt) | copy-start | bytes 98308
  24.5 0.7 %copy-start.16 = (f32[4,8,128]{2,1,0:T(8,128)S(1)}, f32[4,8,128]{2,1,0:T(8,128)}, u32[]{:S(2)}) copy-start(f32[4,8,128]{2,1,0:T(8,128)} %get-tuple-element.30.yt) | copy-start | bytes 49156
  32.3 0.6 %copy-start.14 = (f32[2,32,128]{2,1,0:T(8,128)}, f32[2,32,128]{2,1,0:T(8,128)S(1)}, u32[]{:S(2)}) copy-start(f32[2,32,128]{2,1,0:T(8,128)S(1)} %get-tuple-element.38.coarse) | copy-start | bytes 98308
  32.9 0.6 %copy-start.15 = (f32[2,32,128]{2,1,0:T(8,128)}, f32[2,32,128]{2,1,0:T(8,128)S(1)}, u32[]{:S(2)}) copy-start(f32[2,32,128]{2,1,0:T(8,128)S(1)} %get-tuple-element.39.sx) | copy-start | bytes 98308
  33.5 0.6 %copy-start.17 = (f32[2,2,128]{2,1,0:T(2,128)}, f32[2,2,128]{2,1,0:T(2,128)S(1)}, u32[]{:S(2)}) copy-start(f32[2,2,128]{2,1,0:T(2,128)S(1)} %get-tuple-element.40.sy) | copy-start | bytes 6148

commit v2 on v1

--- a/solution.py
+++ b/solution.py
@@ -405,7 +405,7 @@
 def body(pressure, sat_water, sat_gas, pore_volume, mass_old, transmissibility, upwind):
     nx, ny, nz = pressure.shape
     f32, i32 = jnp.float32, jnp.int32
-    anywhere = pl.BlockSpec(memory_space=pl.ANY)
+    anywhere = pl.BlockSpec(memory_space=pltpu.HBM)
     in_vmem = pl.BlockSpec(memory_space=pltpu.VMEM)
     shape = jax.ShapeDtypeStruct
     halos = pl.pallas_call(

time: 44.4 us -> 44.4 us (level)
  no operation moved by 1% of the time
where the time goes in v2:
time: 44.4 us; the launch traced here: 43.6 us
  Pallas kernels  26.3 us (59%)
  local copies, waits for them, and re-layouts  16.6 us (37%)
  between operations  0.69 us (2%)
    unnamed x37, local copies, waits for them, and re-layouts  16.6 us
    pallas_call x1, Pallas kernels, body(): pl.pallas_call(halo_kernel, out_shape=[shape((3, ny, nz), f32), shape((3,...  11.1 us
    pallas_call x1, Pallas kernels, body(): pl.pallas_call(share_kernel, out_shape=shape(coarse.shape, f32), in_specs...  8.09 us
    pallas_call x1, Pallas kernels, body(): pl.pallas_call(main_kernel, out_shape=[shape(k + grid, f32) for k in lead...  7.11 us

profile of v2, /device:TPU:0, one launch (start us, length us, event | category | flops | bytes accessed | tf_op | source)
XLA Modules:
  0.0 43.6 jit_solution(7733652135279183224)
XLA Ops:
  0.6 11.1 %halo.1 = (f32[3,64,128]{2,1,0:T(8,128)}, f32[3,64,128]{2,1,0:T(8,128)}, f32[64,128]{1,0:T(8,128)}, s32[3,64,128]{2,1,0:T(8,128)}, f32[3,4,8,128]{3,2,1,0:T(8,12...) custom-call(f32[4,64,128]{2,1,0:T(8,128)} %p.3, f32[4,64,128]{2,1,0:T(8,128)} %sw.3, ...), custom_call_target="tpu_custom_call" | custom-call | tf_op jit(solution)/shard_map/halo/pallas_call | solution.py:411
  11.8 0.0 copy-start
  11.8 1.3 %copy-done = s32[3,3,4,64,128]{4,3,2,1,0:T(8,128)S(1)} copy-done((s32[3,3,4,64,128]{4,3,2,1,0:T(8,128)S(1)}, s32[3,3,4,64,128]{4,3,2,1,0:T(8,128)}, u32[]{:S(2)}) %copy-start) | copy-done | bytes 1179672
  13.0 0.0 copy-start.1
  13.0 1.0 %copy-done.1 = f32[3,4,64,128]{3,2,1,0:T(8,128)S(1)} copy-done((f32[3,4,64,128]{3,2,1,0:T(8,128)S(1)}, f32[3,4,64,128]{3,2,1,0:T(8,128)}, u32[]{:S(2)}) %copy-start.1) | copy-done | bytes 393240
  14.0 0.0 copy-start.2
  14.0 0.9 %copy-done.2 = f32[4,64,128]{2,1,0:T(8,128)S(1)} copy-done((f32[4,64,128]{2,1,0:T(8,128)S(1)}, f32[4,64,128]{2,1,0:T(8,128)}, u32[]{:S(2)}) %copy-start.2) | copy-done | bytes 131096
  14.9 0.0 copy-start.3
  14.9 0.9 %copy-done.3 = f32[4,64,128]{2,1,0:T(8,128)S(1)} copy-done((f32[4,64,128]{2,1,0:T(8,128)S(1)}, f32[4,64,128]{2,1,0:T(8,128)}, u32[]{:S(2)}) %copy-start.3) | copy-done | bytes 131096
  15.8 0.0 copy-start.4
  15.8 0.9 %copy-done.4 = f32[4,64,128]{2,1,0:T(8,128)S(1)} copy-done((f32[4,64,128]{2,1,0:T(8,128)S(1)}, f32[4,64,128]{2,1,0:T(8,128)}, u32[]{:S(2)}) %copy-start.4) | copy-done | bytes 131096
  16.7 0.0 copy-start.5
  16.7 1.0 %copy-done.5 = f32[3,4,64,128]{3,2,1,0:T(8,128)S(1)} copy-done((f32[3,4,64,128]{3,2,1,0:T(8,128)S(1)}, f32[3,4,64,128]{3,2,1,0:T(8,128)}, u32[]{:S(2)}) %copy-start.5) | copy-done | bytes 393240
  17.7 0.0 copy-start.6
  17.7 0.9 %copy-done.6 = f32[4,64,128]{2,1,0:T(8,128)S(1)} copy-done((f32[4,64,128]{2,1,0:T(8,128)S(1)}, f32[4,64,128]{2,1,0:T(8,128)}, u32[]{:S(2)}) %copy-start.6) | copy-done | bytes 131096
  18.6 0.0 copy-start.7
  18.6 0.9 %copy-done.7 = f32[3,64,128]{2,1,0:T(8,128)S(1)} copy-done((f32[3,64,128]{2,1,0:T(8,128)S(1)}, f32[3,64,128]{2,1,0:T(8,128)}, u32[]{:S(2)}) %copy-start.7) | copy-done | bytes 98328
  19.5 0.0 copy-start.8
  19.5 0.9 %copy-done.8 = f32[3,64,128]{2,1,0:T(8,128)S(1)} copy-done((f32[3,64,128]{2,1,0:T(8,128)S(1)}, f32[3,64,128]{2,1,0:T(8,128)}, u32[]{:S(2)}) %copy-start.8) | copy-done | bytes 98328
  20.4 0.0 copy-start.9
  20.4 0.9 %copy-done.9 = s32[3,64,128]{2,1,0:T(8,128)S(1)} copy-done((s32[3,64,128]{2,1,0:T(8,128)S(1)}, s32[3,64,128]{2,1,0:T(8,128)}, u32[]{:S(2)}) %copy-start.9) | copy-done | bytes 98328
  21.3 0.0 copy-start.10
  21.3 0.8 %copy-done.10 = f32[3,4,8,128]{3,2,1,0:T(8,128)S(1)} copy-done((f32[3,4,8,128]{3,2,1,0:T(8,128)S(1)}, f32[3,4,8,128]{3,2,1,0:T(8,128)}, u32[]{:S(2)}) %copy-start.10) | copy-done | bytes 49176
  22.1 0.0 copy-start.11
  22.1 0.8 %copy-done.11 = f32[3,4,8,128]{3,2,1,0:T(8,128)S(1)} copy-done((f32[3,4,8,128]{3,2,1,0:T(8,128)S(1)}, f32[3,4,8,128]{3,2,1,0:T(8,128)}, u32[]{:S(2)}) %copy-start.11) | copy-done | bytes 49176
  22.9 0.0 copy-start.12
  22.9 0.8 %copy-done.12 = s32[3,4,8,128]{3,2,1,0:T(8,128)S(1)} copy-done((s32[3,4,8,128]{3,2,1,0:T(8,128)S(1)}, s32[3,4,8,128]{3,2,1,0:T(8,128)}, u32[]{:S(2)}) %copy-start.12) | copy-done | bytes 49176
  23.7 0.0 copy-start.13
  23.7 0.8 %copy-done.13 = f32[64,128]{1,0:T(8,128)S(1)} copy-done((f32[64,128]{1,0:T(8,128)S(1)}, f32[64,128]{1,0:T(8,128)}, u32[]{:S(2)}) %copy-start.13) | copy-done | bytes 32792
  24.5 0.0 copy-start.16
  24.5 0.7 %copy-done.16 = f32[4,8,128]{2,1,0:T(8,128)S(1)} copy-done((f32[4,8,128]{2,1,0:T(8,128)S(1)}, f32[4,8,128]{2,1,0:T(8,128)}, u32[]{:S(2)}) %copy-start.16) | copy-done | bytes 16408
  25.2 7.1 %assemble.1 = (f32[3,4,64,128]{3,2,1,0:T(8,128)}, f32[9,4,64,128]{3,2,1,0:T(8,128)}, f32[3,9,4,64,128]{4,3,2,1,0:T(8,128)}, f32[3,9,4,64,128]{4,3,2,1,0:T(8,128)...) custom-call(f32[4,64,128]{2,1,0:T(8,128)S(1)} %copy-done.2, ...), custom_call_target="tpu_custom_call" | custom-call | tf_op jit(solution)/shard_map/assemble/pallas_call | solution.py:426
  32.3 0.0 copy-start.14
  32.3 0.6 %copy-done.14 = f32[2,32,128]{2,1,0:T(8,128)} copy-done((f32[2,32,128]{2,1,0:T(8,128)}, f32[2,32,128]{2,1,0:T(8,128)S(1)}, u32[]{:S(2)}) %copy-start.14) | copy-done | bytes 32792
  32.9 0.0 copy-start.15
  32.9 0.6 %copy-done.15 = f32[2,32,128]{2,1,0:T(8,128)} copy-done((f32[2,32,128]{2,1,0:T(8,128)}, f32[2,32,128]{2,1,0:T(8,128)S(1)}, u32[]{:S(2)}) %copy-start.15) | copy-done | bytes 32792
  33.5 0.0 copy-start.17
  33.5 0.6 %copy-done.17 = f32[2,2,128]{2,1,0:T(2,128)} copy-done((f32[2,2,128]{2,1,0:T(2,128)}, f32[2,2,128]{2,1,0:T(2,128)S(1)}, u32[]{:S(2)}) %copy-start.17) | copy-done | bytes 2072
  34.1 8.1 %shares.1 = f32[2,32,128]{2,1,0:T(8,128)} custom-call(f32[2,32,128]{2,1,0:T(8,128)} %copy-done.14, f32[2,32,128]{2,1,0:T(8,128)} %copy-done.15, f32[2,2,128]{2,1,0:T(2,128)} %copy-done.17), custom_call_target="tpu_custom_call" | custom-call | tf_op jit(solution)/shard_map/shares/pallas_call | solution.py:454
  42.2 1.4 %copy.15 = f32[2,32,128]{2,1,0:T(8,128)} copy(f32[2,32,128]{2,1,0:T(8,128)} %shares.1) | data formatting | bytes 65536
Async XLA Ops:
  11.8 1.3 %copy-start = (s32[3,3,4,64,128]{4,3,2,1,0:T(8,128)S(1)}, s32[3,3,4,64,128]{4,3,2,1,0:T(8,128)}, u32[]{:S(2)}) copy-start(s32[3,3,4,64,128]{4,3,2,1,0:T(8,128)} %u.3) | copy-start | bytes 3538948
  13.0 1.0 %copy-start.1 = (f32[3,4,64,128]{3,2,1,0:T(8,128)S(1)}, f32[3,4,64,128]{3,2,1,0:T(8,128)}, u32[]{:S(2)}) copy-start(f32[3,4,64,128]{3,2,1,0:T(8,128)} %t.3) | copy-start | bytes 1179652
  14.0 0.9 %copy-start.2 = (f32[4,64,128]{2,1,0:T(8,128)S(1)}, f32[4,64,128]{2,1,0:T(8,128)}, u32[]{:S(2)}) copy-start(f32[4,64,128]{2,1,0:T(8,128)} %p.3) | copy-start | bytes 393220
  14.9 0.9 %copy-start.3 = (f32[4,64,128]{2,1,0:T(8,128)S(1)}, f32[4,64,128]{2,1,0:T(8,128)}, u32[]{:S(2)}) copy-start(f32[4,64,128]{2,1,0:T(8,128)} %sw.3) | copy-start | bytes 393220
  15.8 0.9 %copy-start.4 = (f32[4,64,128]{2,1,0:T(8,128)S(1)}, f32[4,64,128]{2,1,0:T(8,128)}, u32[]{:S(2)}) copy-start(f32[4,64,128]{2,1,0:T(8,128)} %sg.3) | copy-start | bytes 393220
  16.7 1.0 %copy-start.5 = (f32[3,4,64,128]{3,2,1,0:T(8,128)S(1)}, f32[3,4,64,128]{3,2,1,0:T(8,128)}, u32[]{:S(2)}) copy-start(f32[3,4,64,128]{3,2,1,0:T(8,128)} %old.1) | copy-start | bytes 1179652
  17.7 0.9 %copy-start.6 = (f32[4,64,128]{2,1,0:T(8,128)S(1)}, f32[4,64,128]{2,1,0:T(8,128)}, u32[]{:S(2)}) copy-start(f32[4,64,128]{2,1,0:T(8,128)} %pv.1) | copy-start | bytes 393220
  18.6 0.9 %copy-start.7 = (f32[3,64,128]{2,1,0:T(8,128)S(1)}, f32[3,64,128]{2,1,0:T(8,128)}, u32[]{:S(2)}) copy-start(f32[3,64,128]{2,1,0:T(8,128)} %get-tuple-element.24.xlo) | copy-start | bytes 294916
  19.5 0.9 %copy-start.8 = (f32[3,64,128]{2,1,0:T(8,128)S(1)}, f32[3,64,128]{2,1,0:T(8,128)}, u32[]{:S(2)}) copy-start(f32[3,64,128]{2,1,0:T(8,128)} %get-tuple-element.25.xhi) | copy-start | bytes 294916
  20.4 0.9 %copy-start.9 = (s32[3,64,128]{2,1,0:T(8,128)S(1)}, s32[3,64,128]{2,1,0:T(8,128)}, u32[]{:S(2)}) copy-start(s32[3,64,128]{2,1,0:T(8,128)} %get-tuple-element.27.xu) | copy-start | bytes 294916
  21.3 0.8 %copy-start.10 = (f32[3,4,8,128]{3,2,1,0:T(8,128)S(1)}, f32[3,4,8,128]{3,2,1,0:T(8,128)}, u32[]{:S(2)}) copy-start(f32[3,4,8,128]{3,2,1,0:T(8,128)} %get-tuple-element.28.ylo) | copy-start | bytes 147460
  22.1 0.8 %copy-start.11 = (f32[3,4,8,128]{3,2,1,0:T(8,128)S(1)}, f32[3,4,8,128]{3,2,1,0:T(8,128)}, u32[]{:S(2)}) copy-start(f32[3,4,8,128]{3,2,1,0:T(8,128)} %get-tuple-element.29.yhi) | copy-start | bytes 147460
  22.9 0.8 %copy-start.12 = (s32[3,4,8,128]{3,2,1,0:T(8,128)S(1)}, s32[3,4,8,128]{3,2,1,0:T(8,128)}, u32[]{:S(2)}) copy-start(s32[3,4,8,128]{3,2,1,0:T(8,128)} %get-tuple-element.31.yu) | copy-start | bytes 147460
  23.7 0.8 %copy-start.13 = (f32[64,128]{1,0:T(8,128)S(1)}, f32[64,128]{1,0:T(8,128)}, u32[]{:S(2)}) copy-start(f32[64,128]{1,0:T(8,128)} %get-tuple-element.26.xt) | copy-start | bytes 98308
  24.5 0.7 %copy-start.16 = (f32[4,8,128]{2,1,0:T(8,128)S(1)}, f32[4,8,128]{2,1,0:T(8,128)}, u32[]{:S(2)}) copy-start(f32[4,8,128]{2,1,0:T(8,128)} %get-tuple-element.30.yt) | copy-start | bytes 49156
  32.3 0.6 %copy-start.14 = (f32[2,32,128]{2,1,0:T(8,128)}, f32[2,32,128]{2,1,0:T(8,128)S(1)}, u32[]{:S(2)}) copy-start(f32[2,32,128]{2,1,0:T(8,128)S(1)} %get-tuple-element.38.coarse) | copy-start | bytes 98308
  32.9 0.6 %copy-start.15 = (f32[2,32,128]{2,1,0:T(8,128)}, f32[2,32,128]{2,1,0:T(8,128)S(1)}, u32[]{:S(2)}) copy-start(f32[2,32,128]{2,1,0:T(8,128)S(1)} %get-tuple-element.39.sx) | copy-start | bytes 98308
  33.5 0.6 %copy-start.17 = (f32[2,2,128]{2,1,0:T(2,128)}, f32[2,2,128]{2,1,0:T(2,128)S(1)}, u32[]{:S(2)}) copy-start(f32[2,2,128]{2,1,0:T(2,128)S(1)} %get-tuple-element.40.sy) | copy-start | bytes 6148

commit v3 on v2

--- a/solution.py
+++ b/solution.py
@@ -447,7 +447,7 @@
             pltpu.SemaphoreType.DMA((27,)),
             pltpu.SemaphoreType.DMA((ny // ROWS, 6)),
         ],
-        compiler_params=pltpu.CompilerParams(vmem_limit_bytes=40 * 2**20),
+        compiler_params=pltpu.CompilerParams(vmem_limit_bytes=62 * 2**20),
         name="assemble",
     )(pressure, sat_water, sat_gas, pore_volume, mass_old, transmissibility, upwind, *halos)
     *blocks, coarse, sx, sy = results

time: 44.4 us -> 29.4 us (0.66); the launches traced: 43.6 us -> 29.1 us
  local copies, waits for them, and re-layouts: 16.6 us -> 1.38 us
  Pallas kernels: 26.3 us -> 27.1 us
    unnamed x37 -> x1, local copies, waits for them, and re-layouts: 16.6 us -> 1.38 us
    pallas_call x1, Pallas kernels: 7.11 us -> 7.91 us  [body(): pl.pallas_call(main_kernel, out_shape=[shape(k + grid, f32) for k in lead...]
where the time goes in v3:
time: 29.4 us; the launch traced here: 29.1 us
  Pallas kernels  27.1 us (92%)
  local copies, waits for them, and re-layouts  1.38 us (5%)
  between operations  0.66 us (2%)
    pallas_call x1, Pallas kernels, body(): pl.pallas_call(halo_kernel, out_shape=[shape((3, ny, nz), f32), shape((3,...  11.1 us
    pallas_call x1, Pallas kernels, body(): pl.pallas_call(share_kernel, out_shape=shape(coarse.shape, f32), in_specs...  8.08 us
    pallas_call x1, Pallas kernels, body(): pl.pallas_call(main_kernel, out_shape=[shape(k + grid, f32) for k in lead...  7.91 us
    unnamed x1, local copies, waits for them, and re-layouts  1.38 us

profile of v3, /device:TPU:0, one launch (start us, length us, event | category | flops | bytes accessed | tf_op | source)
XLA Modules:
  0.0 29.1 jit_solution(11699190180380959988)
XLA Ops:
  0.6 11.1 %halo.1 = (f32[3,64,128]{2,1,0:T(8,128)}, f32[3,64,128]{2,1,0:T(8,128)}, f32[64,128]{1,0:T(8,128)}, s32[3,64,128]{2,1,0:T(8,128)}, f32[3,4,8,128]{3,2,1,0:T(8,12...) custom-call(f32[4,64,128]{2,1,0:T(8,128)} %p.3, f32[4,64,128]{2,1,0:T(8,128)} %sw.3, ...), custom_call_target="tpu_custom_call" | custom-call | tf_op jit(solution)/shard_map/halo/pallas_call | solution.py:411
  11.8 7.9 %assemble.1 = (f32[3,4,64,128]{3,2,1,0:T(8,128)}, f32[9,4,64,128]{3,2,1,0:T(8,128)}, f32[3,9,4,64,128]{4,3,2,1,0:T(8,128)}, f32[3,9,4,64,128]{4,3,2,1,0:T(8,128)...) custom-call(f32[4,64,128]{2,1,0:T(8,128)} %p.3, ...), custom_call_target="tpu_custom_call" | custom-call | tf_op jit(solution)/shard_map/assemble/pallas_call | solution.py:426
  19.7 8.1 %shares.1 = f32[2,32,128]{2,1,0:T(8,128)} custom-call(f32[2,32,128]{2,1,0:T(8,128)} %get-tuple-element.38.coarse, f32[2,32,128]{2,1,0:T(8,128)} %get-tuple-element.39.sx, f32[2,2,128]{2,1,0:T(2,128)} %get-tuple-element.40.sy), custom_call_target="tpu_custom_call" | custom-call | tf_op jit(solution)/shard_map/shares/pallas_call | solution.py:454
  27.8 1.4 %copy.15 = f32[2,32,128]{2,1,0:T(8,128)} copy(f32[2,32,128]{2,1,0:T(8,128)} %shares.1) | data formatting | bytes 65536

commit v4 on v3

v4 whole, which is shorter than its diff:
```python
import jax
import jax.numpy as jnp
from jax import lax
from jax.experimental import pallas as pl
from jax.experimental.pallas import tpu as pltpu
from jax.sharding import PartitionSpec as P

MESH = pl.DeviceIdType.MESH
ROWS = 8
CHUNK = 16
LIMIT = 24 * 2**20
PLACES = (0, 1, 3, 4, 6, 7, 8)


def neighbours():
    found = []
    for axis in ("gx", "gy"):
        here, size = lax.axis_index(axis), lax.axis_size(axis)
        found.append((axis, here - 1, here > 0))
        found.append((axis, here + 1, here < size - 1))
    return found


def meet():
    barrier = pltpu.get_barrier_semaphore()
    for axis, other, there in neighbours():

        @pl.when(there)
        def _():
            pl.semaphore_signal(barrier, inc=1, device_id={axis: other}, device_id_type=MESH)

    peers = sum(there.astype(jnp.int32) for _, _, there in neighbours())
    pl.semaphore_wait(barrier, peers)


def cell(p, sw, sg):
    so = 1.0 - sw - sg
    bw = 1.0 + 0.05 * p
    bo = 1.0 + 0.1 * p
    ww, oo, gg = sw * sw, so * so, 5.0 * (sg * sg)
    sob = so * bo
    return dict(
        p=p, sw=sw, sg=sg, so=so, bw=bw, bo=bo, sob=sob, rs=0.3 * p,
        m=(2.0 * ww * bw, 0.5 * so * sob, gg * p),
        mp=(0.1 * ww, 0.05 * oo, gg),
        ms=(4.0 * sw * bw, -sob, 10.0 * sg * p),
    )


def face(low, high, t, flags, heads):
    drop = low["p"] - high["p"]
    ups = [flag > 0 for flag in flags]
    flow, by_low, by_high = [], [], []
    for a in range(3):
        drive = t * (drop + heads[a]) if heads[a] else t * drop
        chosen = jnp.where(ups[a], low["m"][a], high["m"][a])
        moved = t * chosen
        flow.append(drive * chosen)
        from_low = jnp.where(ups[a], drive, 0.0)
        from_high = jnp.where(ups[a], 0.0, drive)
        by_low.append((from_low * low["mp"][a] + moved, from_low * low["ms"][a]))
        by_high.append((from_high * high["mp"][a] - moved, from_high * high["ms"][a]))
    solved = jnp.where(ups[1], low["rs"], high["rs"])
    fluxes = [flow[0], flow[1], flow[2] + solved * flow[1]]
    third = 0.3 * flow[1]
    extra_low = jnp.where(ups[1], third, 0.0)
    extra_high = jnp.where(ups[1], 0.0, third)
    out = []
    for (w, o, g), extra in ((by_low, extra_low), (by_high, extra_high)):
        carried = solved * o[1]
        out.append([w[0], w[1], o[0], o[1], g[0] + solved * o[0] + extra, carried, g[1] + carried])
    return fluxes, out[0], out[1]


def column(weight, entries):
    return weight[0] * entries[0] + weight[1] * entries[2] + weight[2] * entries[4]


def put(ref, lead, x, rows, entries, sign=1.0):
    for place, entry in zip(PLACES, entries):
        ref[lead + (place, x, rows)] = entry if sign > 0 else -entry
    ref[lead + (2, x, rows)] = jnp.zeros_like(entries[0])
    ref[lead + (5, x, rows)] = entries[3] if sign > 0 else -entries[3]


def main_kernel(
    p, sw, sg, pv, old, t, u,
    res_v, diag_v, low_v, up_v, rows_v, pro_v, coarse_o,
    ps, pvs, olds, txs, tys, tzs, uxs, uys, uzs,
    own_s, side_s, sx, sy, gx_in, gy_in,
    in_sem, xs_sem, xr_sem, ys_sem, yr_sem, share_s, share_r,
):
    nx, ny, nz = p.shape
    chunks = ny // CHUNK
    inner = pl.ds(ROWS, ny)
    mid = pl.ds(1, nx)
    states_in = (p, sw, sg)
    pairs = [(s, ps.at[i, mid, inner]) for i, s in enumerate(states_in)]
    pairs += [
        (pv, pvs), (old, olds), (t.at[0], txs.at[pl.ds(0, nx)]), (t.at[1], tys.at[:, pl.ds(0, ny)]),
        (t.at[2], tzs), (u.at[0], uxs.at[:, pl.ds(0, nx)]), (u.at[1], uys.at[:, :, pl.ds(0, ny)]),
        (u.at[2], uzs),
    ]
    local = [pltpu.make_async_copy(a, b, in_sem.at[k]) for k, (a, b) in enumerate(pairs)]
    for copy in local:
        copy.start()

    (_, xl, has_xl), (_, xh, has_xh), (_, yl, has_yl), (_, yh, has_yh) = neighbours()

    def remote(pairs, send, recv, axis, other, base):
        return [
            pltpu.make_async_remote_copy(
                src_ref=a, dst_ref=b, send_sem=send(base + k), recv_sem=recv(base + k),
                device_id={axis: other}, device_id_type=MESH,
            )
            for k, (a, b) in enumerate(pairs)
        ]

    def x_copies(c):
        begin = pl.multiple_of(c * CHUNK, CHUNK)
        rows = pl.ds(begin, CHUNK)
        put_rows = pl.ds(pl.multiple_of(begin + ROWS, ROWS), CHUNK)
        up = [(s.at[nx - 1, rows], ps.at[i, 0, put_rows]) for i, s in enumerate(states_in)]
        down = [(s.at[0, rows], ps.at[i, nx + 1, put_rows]) for i, s in enumerate(states_in)]
        down += [(t.at[0, 0, rows], txs.at[nx, rows]), (u.at[0, :, 0, rows], uxs.at[:, nx, rows])]
        send, recv = (lambda k: xs_sem.at[c, k]), (lambda k: xr_sem.at[c, k])
        return remote(up, send, recv, "gx", xh, 0), remote(down, send, recv, "gx", xl, 3)

    first, last, beyond = pl.ds(0, ROWS), pl.ds(ny - ROWS, ROWS), pl.ds(ny + ROWS, ROWS)
    up = [(s.at[:, last], ps.at[i, mid, first]) for i, s in enumerate(states_in)]
    down = [(s.at[:, first], ps.at[i, mid, beyond]) for i, s in enumerate(states_in)]
    down += [(t.at[1, :, first], tys.at[:, pl.ds(ny, ROWS)]), (u.at[1, :, :, first], uys.at[:, :, pl.ds(ny, ROWS)])]
    y_up = remote(up, lambda k: ys_sem.at[k], lambda k: yr_sem.at[k], "gy", yh, 0)
    y_down = remote(down, lambda k: ys_sem.at[k], lambda k: yr_sem.at[k], "gy", yl, 3)

    def when(there, copies, what):
        @pl.when(there)
        def _():
            for copy in copies:
                getattr(copy, what)()

    meet()

    def begin(c, carry):
        x_up, x_down = x_copies(c)
        when(has_xl, x_down, "start")
        when(has_xh, x_up, "start")
        return carry

    lax.fori_loop(0, 1, begin, 0)
    when(has_yl, y_down, "start")
    when(has_yh, y_up, "start")
    lax.fori_loop(1, chunks, begin, 0)
    none_there = jnp.logical_not

    @pl.when(none_there(has_xl))
    def _():
        ps[:, 0] = jnp.zeros((3, ny + 2 * ROWS, nz), jnp.float32)

    @pl.when(none_there(has_xh))
    def _():
        ps[:, nx + 1] = jnp.zeros((3, ny + 2 * ROWS, nz), jnp.float32)
        txs[nx] = jnp.zeros((ny, nz), jnp.float32)
        uxs[:, nx] = jnp.zeros((3, ny, nz), jnp.int32)

    @pl.when(none_there(has_yl))
    def _():
        ps[:, 1 : nx + 1, 0:ROWS] = jnp.zeros((3, nx, ROWS, nz), jnp.float32)

    @pl.when(none_there(has_yh))
    def _():
        ps[:, 1 : nx + 1, ny + ROWS :] = jnp.zeros((3, nx, ROWS, nz), jnp.float32)
        tys[:, ny:] = jnp.zeros((nx, ROWS, nz), jnp.float32)
        uys[:, :, ny:] = jnp.zeros((3, nx, ROWS, nz), jnp.int32)

    for copy in local:
        copy.wait()

    @pl.when(none_there(has_xl))
    def _():
        txs[0] = jnp.zeros((ny, nz), jnp.float32)

    @pl.when(none_there(has_yl))
    def _():
        tys[:, 0:1] = jnp.zeros((nx, 1, nz), jnp.float32)

    when(has_yh, y_down, "wait_recv")
    when(has_yl, y_up, "wait_recv")

    side_s[:, 0:ROWS] = jnp.zeros((nx // 2, ROWS, nz), jnp.float32)
    side_s[:, ny + ROWS :] = jnp.zeros((nx // 2, ROWS, nz), jnp.float32)

    lane = lax.broadcasted_iota(jnp.int32, (ROWS, nz), 1)
    odd = lax.broadcasted_iota(jnp.int32, (ROWS, nz), 0) % 2 == 1
    flat, depth = (0.0, 0.0, 0.0), (0.1, 0.08, 0.02)
    def step(j, carry):
        start = pl.multiple_of(j * ROWS, ROWS)
        rows = pl.ds(start, ROWS)
        here = pl.ds(pl.multiple_of(start + ROWS, ROWS), ROWS)
        before = pl.ds(start + ROWS - 1, ROWS)
        after = pl.ds(start + ROWS + 1, ROWS)
        following = pl.ds(start + 1, ROWS)

        def states(x, where):
            return [ps[i, x, where] for i in range(3)]

        def x_face(x, low, high):
            return face(low, high, txs[x, rows], [uxs[a, x, rows] for a in range(3)], flat)

        below, centre = cell(*states(0, here)), cell(*states(1, here))
        x_low = x_face(0, below, centre)
        agg = [None] * (nx // 2)
        side = [None] * (nx // 2)

        def add(items, place, value):
            items[place] = value if items[place] is None else items[place] + value

        for x in range(nx):
            above = cell(*states(x + 2, here))
            x_up = x_face(x + 1, centre, above)
            y_low = face(
                cell(*states(x + 1, before)), centre, tys[x, rows],
                [uys[a, x, rows] for a in range(3)], flat,
            )
            y_up = face(
                centre, cell(*states(x + 1, after)), tys[x, following],
                [uys[a, x, following] for a in range(3)], flat,
            )
            under = cell(*[pltpu.roll(centre[n], 1, 1) for n in ("p", "sw", "sg")])
            z_t = jnp.where(lane > 0, tzs[x, rows], 0.0)
            z_low = face(under, centre, z_t, [uzs[a, x, rows] for a in range(3)], depth)
            z_up = [[pltpu.roll(v, nz - 1, 1) for v in part] for part in z_low]
            lows, ups = (x_low, y_low, z_low), (x_up, y_up, z_up)

            c = centre
            pore = pvs[x, rows]
            phi = pore + 0.02 * pore * c["p"]
            dphi = 0.02 * pore
            water, oil = c["bw"] * c["sw"], c["sob"]
            gas = c["p"] * c["sg"] + c["rs"] * oil
            pob = phi * c["bo"]
            rob = c["rs"] * pob
            acc = [
                dphi * water + 0.05 * phi * c["sw"],
                phi * c["bw"],
                dphi * oil + 0.1 * phi * c["so"],
                -pob,
                dphi * gas + phi * (c["sg"] + 0.3 * oil + 0.1 * c["rs"] * c["so"]),
                -rob,
                phi * c["p"] - rob,
            ]
            acc = [2.0 * v for v in acc]
            mass = (phi * water, phi * oil, phi * gas)
            residual = []
            for k in range(3):
                r = 2.0 * (mass[k] - olds[k, x, rows])
                for d in range(3):
                    r = r - lows[d][0][k] + ups[d][0][k]
                res_v[k, x, rows] = r
                residual.append(r)
            diag = []
            for k in range(7):
                v = acc[k]
                for d in range(3):
                    v = v - lows[d][2][k] + ups[d][1][k]
                diag.append(v)
            put(diag_v, (), x, rows, diag)
            for d in range(3):
                put(low_v, (d,), x, rows, lows[d][1], -1.0)
                put(up_v, (d,), x, rows, ups[d][2])

            weight = (1.0 / c["bw"], 1.0 / c["bo"] - 0.3, 1.0 / c["p"])
            p_diag = column(weight, diag)
            p_low = [-column(weight, lows[d][1]) for d in range(3)]
            p_up = [column(weight, ups[d][2]) for d in range(3)]
            divisor = jnp.abs(p_diag) + column(weight, acc)
            for v in p_low + p_up:
                divisor = divisor + jnp.abs(v)
            scale = (2.0 / 3.0) / divisor
            for k, v in enumerate([p_diag] + p_low + p_up):
                rows_v[k, x, rows] = v
            y_same = jnp.where(odd, p_low[1], p_up[1])
            y_low_other = jnp.where(odd, 0.0, p_low[1])
            y_up_other = jnp.where(odd, p_up[1], 0.0)
            x_same, x_other = (p_low[0], p_up[0]) if x % 2 else (p_up[0], p_low[0])
            own = 1.0 - scale * (p_diag + x_same + y_same)
            minus = -scale
            w_x = minus * x_other
            w_yl, w_yu = minus * y_low_other, minus * y_up_other
            w_zl, w_zu = minus * p_low[2], minus * p_up[2]
            none = jnp.zeros_like(own)
            w_xl, w_xu = (none, w_x) if x % 2 else (w_x, none)
            for k, v in enumerate((own, w_xl, w_yl, w_zl, w_xu, w_yu, w_zu)):
                pro_v[k, x, rows] = v

            reduced = weight[0] * residual[0] + weight[1] * residual[1] + weight[2] * residual[2]
            local = own * reduced + pltpu.roll(w_zl * reduced, nz - 1, 1) + pltpu.roll(w_zu * reduced, 1, 1)
            add(agg, x // 2, local)
            add(side, x // 2, (w_yl + w_yu) * reduced)
            share = w_x * reduced
            if x == 0:
                own_s[nx // 2, rows] = share
            elif x == nx - 1:
                own_s[nx // 2 + 1, rows] = share
            else:
                add(agg, (x + 1) // 2 if x % 2 else (x - 1) // 2, share)
            x_low, centre = x_up, above
        for a in range(nx // 2):
            own_s[a, rows] = agg[a]
            side_s[a, here] = side[a]
        return carry

    per = CHUNK // ROWS

    def chunk(c, carry):
        x_up, x_down = x_copies(c)
        when(has_xl, x_up, "wait_recv")
        when(has_xh, x_down, "wait_recv")
        return lax.fori_loop(c * per, (c + 1) * per, step, carry)

    lax.fori_loop(0, chunks, chunk, 0)

    half = ny // 2
    for s in range(2):
        sx[s] = own_s[nx // 2 + s, pl.ds(0, half, stride=2)] + own_s[nx // 2 + s, pl.ds(1, half, stride=2)]
    for a in range(nx // 2):
        sy[0, a : a + 1] = side_s[a, ROWS : ROWS + 1]
        sy[1, a : a + 1] = side_s[a, ROWS + ny - 1 : ROWS + ny]
    routes = (
        (sx.at[0], gx_in.at[0], "gx", xl, has_xl, has_xh),
        (sx.at[1], gx_in.at[1], "gx", xh, has_xh, has_xl),
        (sy.at[0], gy_in.at[0], "gy", yl, has_yl, has_yh),
        (sy.at[1], gy_in.at[1], "gy", yh, has_yh, has_yl),
    )
    shares = []
    for k, (source, target, axis, other, sends, gets) in enumerate(routes):
        copy = remote([(source, target)], lambda n: share_s.at[n], lambda n: share_r.at[n], axis, other, k)
        shares.append(copy)
        when(sends, copy, "start")
    for a in range(nx // 2):
        coarse_o[a] = (
            own_s[a, pl.ds(0, half, stride=2)]
            + own_s[a, pl.ds(1, half, stride=2)]
            + side_s[a, pl.ds(ROWS + 2, half, stride=2)]
            + side_s[a, pl.ds(ROWS - 1, half, stride=2)]
        )
    when(has_yl, y_down, "wait_send")
    when(has_yh, y_up, "wait_send")

    def sent(c, carry):
        x_up, x_down = x_copies(c)
        when(has_xl, x_down, "wait_send")
        when(has_xh, x_up, "wait_send")
        return carry

    lax.fori_loop(0, chunks, sent, 0)
    for k, (source, target, axis, other, sends, gets) in enumerate(routes):
        when(gets, shares[k], "wait_recv")

        @pl.when(gets)
        def _():
            if k == 0:
                coarse_o[nx // 2 - 1] += gx_in[0]
            elif k == 1:
                coarse_o[0] += gx_in[1]
            else:
                place = half - 1 if k == 2 else 0
                for a in range(nx // 2):
                    coarse_o[a, place : place + 1] += gy_in[k - 2, a : a + 1]

        when(sends, shares[k], "wait_send")


def store_kernel(*refs):
    count = len(refs) // 2
    sem = refs[-1]
    copies = [pltpu.make_async_copy(refs[k], refs[count + k], sem.at[k]) for k in range(count)]
    for copy in copies:
        copy.start()
    for copy in copies:
        copy.wait()


def body(pressure, sat_water, sat_gas, pore_volume, mass_old, transmissibility, upwind):
    nx, ny, nz = pressure.shape
    f32, i32 = jnp.float32, jnp.int32
    anywhere = pl.BlockSpec(memory_space=pltpu.HBM)
    in_vmem = pl.BlockSpec(memory_space=pltpu.VMEM)
    shape = jax.ShapeDtypeStruct
    grid = (nx, ny, nz)
    lead = ((3,), (9,), (3, 9), (3, 9), (7,), (7,))
    outs = [shape(k + grid, f32) for k in lead] + [shape((nx // 2, ny // 2, nz), f32)]
    dma = pltpu.SemaphoreType.DMA
    results = pl.pallas_call(
        main_kernel,
        out_shape=[pltpu.VMEM(o.shape, o.dtype) for o in outs],
        in_specs=[anywhere] * 7,
        out_specs=[in_vmem] * 7,
        scratch_shapes=[
            pltpu.VMEM((3, nx + 2, ny + 2 * ROWS, nz), f32),
            pltpu.VMEM(grid, f32),
            pltpu.VMEM((3,) + grid, f32),
            pltpu.VMEM((nx + 1, ny, nz), f32),
            pltpu.VMEM((nx, ny + ROWS, nz), f32),
            pltpu.VMEM(grid, f32),
            pltpu.VMEM((3, nx + 1, ny, nz), i32),
            pltpu.VMEM((3, nx, ny + ROWS, nz), i32),
            pltpu.VMEM((3,) + grid, i32),
            pltpu.VMEM((nx // 2 + 2, ny, nz), f32),
            pltpu.VMEM((nx // 2, ny + 2 * ROWS, nz), f32),
            pltpu.VMEM((2, ny // 2, nz), f32), pltpu.VMEM((2, nx // 2, nz), f32),
            pltpu.VMEM((2, ny // 2, nz), f32), pltpu.VMEM((2, nx // 2, nz), f32),
            dma((11,)), dma((ny // CHUNK, 8)), dma((ny // CHUNK, 8)), dma((8,)), dma((8,)), dma((4,)), dma((4,)),
        ],
        compiler_params=pltpu.CompilerParams(
            collective_id=0, has_side_effects=True, vmem_limit_bytes=LIMIT
        ),
        name="assemble",
    )(*[
        pltpu.with_memory_space_constraint(v, pltpu.HBM)
        for v in (pressure, sat_water, sat_gas, pore_volume, mass_old, transmissibility, upwind)
    ])
    return pl.pallas_call(
        store_kernel,
        out_shape=outs,
        in_specs=[in_vmem] * 7,
        out_specs=[anywhere] * 7,
        scratch_shapes=[dma((7,))],
        compiler_params=pltpu.CompilerParams(vmem_limit_bytes=LIMIT),
        name="store",
    )(*results)


def solution(mesh):
    cells = P("gx", "gy", None)
    one = P(None, "gx", "gy", None)
    two = P(None, None, "gx", "gy", None)
    return jax.shard_map(
        body,
        mesh=mesh,
        in_specs=(cells, cells, cells, cells, one, one, two),
        out_specs=(one, one, two, two, one, one, cells),
        check_vma=False,
    )
```

time: 29.4 us -> 22.9 us (0.78)
  Pallas kernels: 27.1 us -> 22.1 us
  local copies, waits for them, and re-layouts: 1.38 us -> 0 us
    pallas_call x3 -> x2, Pallas kernels: 27.1 us -> 22.1 us  [the longest x1 18.1 us: body(): pl.pallas_call(main_kernel, out_shape=[pltpu.VMEM(o.shape, o.dtype) for o...]
    unnamed x1 -> x0, local copies, waits for them, and re-layouts: 1.38 us -> none
where the time goes in v4:
time: 22.9 us; the launch traced here: 22.7 us
  Pallas kernels  22.1 us (97%)
  between operations  0.64 us (3%)
    pallas_call x1, Pallas kernels, body(): pl.pallas_call(main_kernel, out_shape=[pltpu.VMEM(o.shape, o.dtype) for o...  18.1 us
    pallas_call x1, Pallas kernels, body(): pl.pallas_call(store_kernel, out_shape=outs, in_specs=[in_vmem] * 7, out_...  4.01 us

profile of v4, /device:TPU:0, one launch (start us, length us, event | category | flops | bytes accessed | tf_op | source)
XLA Modules:
  0.0 22.7 jit_solution(8816614797191460049)
XLA Ops:
  0.6 18.1 %assemble.1 = (f32[3,4,64,128]{3,2,1,0:T(8,128)S(1)}, f32[9,4,64,128]{3,2,1,0:T(8,128)S(1)}, f32[3,9,4,64,128]{4,3,2,1,0:T(8,128)S(1)}, f32[3,9,4,64,128]{4,3,2,...) custom-call(f32[4,64,128]{2,1,0:T(8,128)} %p.1, ...), custom_call_target="tpu_custom_call" | custom-call | tf_op jit(solution)/shard_map/assemble/pallas_call | solution.py:394
  18.7 4.0 %store.1 = (f32[3,4,64,128]{3,2,1,0:T(8,128)}, f32[9,4,64,128]{3,2,1,0:T(8,128)}, f32[3,9,4,64,128]{4,3,2,1,0:T(8,128)}, f32[3,9,4,64,128]{4,3,2,1,0:T(8,128)}, ...) custom-call(f32[3,4,64,128]{3,2,1,0:T(8,128)S(1)} %get-tuple-element.14.refs_0_, ...), custom_call_target="tpu_custom_call" | custom-call | tf_op jit(solution)/shard_map/store/pallas_call | solution.py:423
